TPU v7x, 32 devices: a whole 2x2x4 slice. The times are simulated.
32 devices in a mesh: dp: 8 (over y, x, core), mp: 4 (over z).
Axes of the slice: x: 2, y: 2, z: 4, core: 2. Of those that a mesh axis runs over, the one named last changes fastest.
Arguments:
- tokens: bfloat16 [6272, 768], P('dp', 'mp'), may hold values from -6 to 6
- norm_params: float32 [4, 768], replicated, may hold values from -0.3 to 1.5
- w_qkv: float32 [3, 768, 768], P(None, 'dp', 'mp'), may hold values from -0.21875 to 0.21875
- w_proj: float32 [768, 768], P('mp', 'dp'), may hold values from -2.5 to 2.5
- phi: float32 [768, 16], replicated, may hold values from -0.109375 to 0.109375
- w_in: float32 [16, 768, 3072], P('dp', None, 'mp'), may hold values from -3.5 to 3.5
- w_out: float32 [16, 3072, 768], P('dp', 'mp'), may hold values from -0.4375 to 0.4375
- cotangent: bfloat16 [6272, 768], P('dp', 'mp'), may hold values from -6 to 6
Outputs:
- output: float32 [6272, 768], P('dp', 'mp')
- input_grad: float32 [6272, 768], P('dp', 'mp')
- qkv_grad: float32 [3, 768, 768], P(None, 'dp', 'mp')
- proj_grad: float32 [768, 768], P('mp', 'dp')
- expert_in_grad: float32 [16, 768, 3072], P('dp', None, 'mp')
- expert_out_grad: float32 [16, 3072, 768], P('dp', 'mp')
- phi_grad: float32 [768, 16], replicated
- norm_grad: float32 [4, 768], replicated
All inputs are finite; a program needn't handle non-finite values.
Results may differ from a plain program's by a relative error of at most 0.017.
The roundings to bfloat16 on the way count: a program that leaves them out, or rounds other values in their place, can miss the bound.
Values may be sent and summed in bfloat16 or wider, within the bound.
A program may use at most 128 MiB of HBM per device.

v0:
```python
import math

import jax
import jax.numpy as jnp
from jax import lax
from jax.sharding import PartitionSpec as P

D = 768
HEADS = 12
HEAD_DIM = 64
SEQ = 196


EPSILON = 1e-06


def normalize(values_in):
    row_mean = jnp.mean(values_in, axis=-1, keepdims=True)
    centered = values_in - row_mean
    row_var = jnp.mean(centered * centered, axis=-1, keepdims=True)
    inv_std = lax.rsqrt(row_var + EPSILON)
    return (centered * inv_std, inv_std)


def norm_backward(grad_norm_out, gain_row, normed, inv_std):
    scaled = grad_norm_out * gain_row
    first_mean = jnp.mean(scaled, axis=-1, keepdims=True)
    second_mean = jnp.mean(scaled * normed, axis=-1, keepdims=True)
    return inv_std * (scaled - first_mean - normed * second_mean)


def exact_gelu(values_in):
    return jax.nn.gelu(values_in, approximate=False)


def per_device(tokens, norm_params, w_qkv, w_proj, phi, w_in, w_out, cotangent):
    mp_width = lax.axis_size("mp")
    column = lax.axis_index("mp")
    local_cols = tokens.shape[1]
    rows_full, grad_full = (
        lax.all_gather(tokens, "mp", axis=1, tiled=True),
        lax.all_gather(cotangent, "mp", axis=1, tiled=True),
    )
    token_count = rows_full.shape[0]
    images = token_count // SEQ
    heads_local = HEADS // mp_width
    local_width = heads_local * HEAD_DIM
    scale = 1.0 / math.sqrt(HEAD_DIM)
    inputs_f = rows_full.astype(jnp.float32)
    norm_one, inv_one = normalize(inputs_f)
    first = (norm_one * norm_params[0] + norm_params[1]).astype(jnp.bfloat16)
    qkv_local = w_qkv.astype(jnp.bfloat16)
    proj_local = w_proj.astype(jnp.bfloat16)
    qkv_w, proj_w = (
        lax.all_gather(qkv_local, "dp", axis=1, tiled=True),
        lax.all_gather(proj_local, "dp", axis=1, tiled=True),
    )
    projected = jnp.einsum("td,cde->cte", first, qkv_w, preferred_element_type=jnp.float32).astype(
        jnp.bfloat16
    )
    projected = projected.reshape(3, images, SEQ, heads_local, HEAD_DIM)
    query_rows = projected[0]
    key_rows = projected[1]
    value_rows = projected[2]
    scores = (
        jnp.einsum("bqhd,bkhd->bhqk", query_rows, key_rows, preferred_element_type=jnp.float32)
        * scale
    )
    top_score = jnp.max(scores, axis=-1, keepdims=True)
    log_total = top_score + jnp.log(jnp.sum(jnp.exp(scores - top_score), axis=-1, keepdims=True))
    attn_probs = jnp.exp(scores - log_total)
    probs_low = attn_probs.astype(jnp.bfloat16)
    attended = jnp.einsum(
        "bhqk,bkhd->bqhd", probs_low, value_rows, preferred_element_type=jnp.float32
    )
    attended = attended.astype(jnp.bfloat16).reshape(token_count, local_width)
    branch_part = jnp.dot(attended, proj_w, preferred_element_type=jnp.float32)
    branch = lax.psum(branch_part, "mp")
    residual = inputs_f + branch
    norm_two, inv_two = normalize(residual)
    second = (norm_two * norm_params[2] + norm_params[3]).astype(jnp.bfloat16)
    phi_low = phi.astype(jnp.bfloat16)
    experts = phi.shape[1]
    logits = jnp.dot(second, phi_low, preferred_element_type=jnp.float32).reshape(
        images, SEQ, experts
    )
    dispatch = jax.nn.softmax(logits, axis=1)
    combine = jax.nn.softmax(logits, axis=2)
    dispatch_low = dispatch.astype(jnp.bfloat16)
    combine_low = combine.astype(jnp.bfloat16)
    second_img = second.reshape(images, SEQ, D)
    slot_rows = jnp.einsum(
        "bse,bsd->bed", dispatch_low, second_img, preferred_element_type=jnp.float32
    ).astype(jnp.bfloat16)
    expert_slots = lax.all_to_all(slot_rows, "dp", split_axis=1, concat_axis=0, tiled=True)
    w_in_low = w_in.astype(jnp.bfloat16)
    w_out_low = w_out.astype(jnp.bfloat16)
    pre_act = jnp.einsum("red,edf->ref", expert_slots, w_in_low, preferred_element_type=jnp.float32)
    hidden = exact_gelu(pre_act).astype(jnp.bfloat16)
    result_part = jnp.einsum("ref,efd->red", hidden, w_out_low, preferred_element_type=jnp.float32)
    results = lax.psum(result_part, "mp").astype(jnp.bfloat16)
    results_img = lax.all_to_all(results, "dp", split_axis=0, concat_axis=1, tiled=True)
    moe_mixed = jnp.einsum(
        "bse,bed->bsd", combine_low, results_img, preferred_element_type=jnp.float32
    )
    output_full = residual + moe_mixed.reshape(token_count, D)
    output = lax.dynamic_slice_in_dim(output_full, column * local_cols, local_cols, 1)
    grad_img = grad_full.reshape(images, SEQ, D)
    grad_combine = jnp.einsum(
        "bsd,bed->bse", grad_img, results_img, preferred_element_type=jnp.float32
    )
    grad_results = jnp.einsum(
        "bse,bsd->bed", combine_low, grad_img, preferred_element_type=jnp.float32
    ).astype(jnp.bfloat16)
    grad_expert = lax.all_to_all(grad_results, "dp", split_axis=1, concat_axis=0, tiled=True)
    grad_hidden = jnp.einsum(
        "red,efd->ref", grad_expert, w_out_low, preferred_element_type=jnp.float32
    )
    unused_value, gelu_back = jax.vjp(exact_gelu, pre_act)
    grad_pre = gelu_back(grad_hidden)[0].astype(jnp.bfloat16)
    expert_out_grad = jnp.einsum(
        "ref,red->efd", hidden, grad_expert, preferred_element_type=jnp.float32
    )
    expert_in_grad = jnp.einsum(
        "red,ref->edf", expert_slots, grad_pre, preferred_element_type=jnp.float32
    )
    slot_grad_part = jnp.einsum(
        "ref,edf->red", grad_pre, w_in_low, preferred_element_type=jnp.float32
    )
    slot_grad = lax.psum(slot_grad_part, "mp").astype(jnp.bfloat16)
    slot_grad_img = lax.all_to_all(slot_grad, "dp", split_axis=0, concat_axis=1, tiled=True)
    grad_dispatch = jnp.einsum(
        "bsd,bed->bse", second_img, slot_grad_img, preferred_element_type=jnp.float32
    )
    grad_second = jnp.einsum(
        "bse,bed->bsd", dispatch_low, slot_grad_img, preferred_element_type=jnp.float32
    )
    grad_logits = dispatch * (
        grad_dispatch - jnp.sum(dispatch * grad_dispatch, axis=1, keepdims=True)
    )
    grad_logits = grad_logits + combine * (
        grad_combine - jnp.sum(combine * grad_combine, axis=2, keepdims=True)
    )
    logits_low = grad_logits.reshape(token_count, experts).astype(jnp.bfloat16)
    grad_second = grad_second.reshape(token_count, D) + jnp.einsum(
        "te,de->td", logits_low, phi_low, preferred_element_type=jnp.float32
    )
    phi_part = jnp.einsum("td,te->de", second, logits_low, preferred_element_type=jnp.float32)
    grad_residual = grad_full.astype(jnp.float32) + norm_backward(
        grad_second, norm_params[2], norm_two, inv_two
    )
    qkv_back, proj_back = (
        lax.all_gather(qkv_local, "dp", axis=1, tiled=True),
        lax.all_gather(proj_local, "dp", axis=1, tiled=True),
    )
    branch_grad = grad_residual.astype(jnp.bfloat16)
    proj_part = jnp.einsum("tc,td->cd", attended, branch_grad, preferred_element_type=jnp.float32)
    grad_attended = jnp.einsum(
        "td,cd->tc", branch_grad, proj_back, preferred_element_type=jnp.float32
    )
    grad_attended = grad_attended.astype(jnp.bfloat16).reshape(images, SEQ, heads_local, HEAD_DIM)
    scores_again = (
        jnp.einsum("bqhd,bkhd->bhqk", query_rows, key_rows, preferred_element_type=jnp.float32)
        * scale
    )
    probs_again = jnp.exp(scores_again - log_total)
    probs_again_low = probs_again.astype(jnp.bfloat16)
    grad_probs = jnp.einsum(
        "bqhd,bkhd->bhqk", grad_attended, value_rows, preferred_element_type=jnp.float32
    )
    grad_scores = probs_again * (
        grad_probs - jnp.sum(probs_again * grad_probs, axis=-1, keepdims=True)
    )
    grad_scores = grad_scores.astype(jnp.bfloat16)
    grad_query = (
        jnp.einsum("bhqk,bkhd->bqhd", grad_scores, key_rows, preferred_element_type=jnp.float32)
        * scale
    )
    grad_key = (
        jnp.einsum("bhqk,bqhd->bkhd", grad_scores, query_rows, preferred_element_type=jnp.float32)
        * scale
    )
    grad_value = jnp.einsum(
        "bhqk,bqhd->bkhd", probs_again_low, grad_attended, preferred_element_type=jnp.float32
    )
    grad_qkv = (
        jnp.stack([grad_query, grad_key, grad_value])
        .astype(jnp.bfloat16)
        .reshape(3, token_count, local_width)
    )
    qkv_part = jnp.einsum("td,cte->cde", first, grad_qkv, preferred_element_type=jnp.float32)
    first_grad_part = jnp.einsum(
        "cte,cde->td", grad_qkv, qkv_back, preferred_element_type=jnp.float32
    )
    grad_first = lax.psum(first_grad_part, "mp")
    input_full = grad_residual + norm_backward(grad_first, norm_params[0], norm_one, inv_one)
    input_grad = lax.dynamic_slice_in_dim(input_full, column * local_cols, local_cols, 1)
    qkv_grad, proj_grad = (
        lax.psum_scatter(qkv_part, "dp", scatter_dimension=1, tiled=True),
        lax.psum_scatter(proj_part, "dp", scatter_dimension=1, tiled=True),
    )
    norm_part = jnp.stack(
        [
            jnp.sum(grad_first * norm_one, axis=0),
            jnp.sum(grad_first, axis=0),
            jnp.sum(grad_second * norm_two, axis=0),
            jnp.sum(grad_second, axis=0),
        ]
    )
    phi_grad, norm_grad = lax.psum((phi_part, norm_part), "dp")
    return (
        output,
        input_grad,
        qkv_grad,
        proj_grad,
        expert_in_grad,
        expert_out_grad,
        phi_grad,
        norm_grad,
    )


def solution(mesh):
    placed = (
        P("dp", "mp"),
        P(),
        P(None, "dp", "mp"),
        P("mp", "dp"),
        P(),
        P("dp", None, "mp"),
        P("dp", "mp", None),
        P("dp", "mp"),
    )
    return jax.shard_map(
        per_device,
        mesh=mesh,
        in_specs=placed,
        out_specs=(
            P("dp", "mp"),
            P("dp", "mp"),
            P(None, "dp", "mp"),
            P("mp", "dp"),
            P("dp", None, "mp"),
            P("dp", "mp", None),
            P(),
            P(),
        ),
        check_vma=False,
    )
```

profile of v0, /device:TPU:0, one launch (start us, length us, event | category | flops | bytes accessed | tf_op | source)
XLA Modules:
  0.0 485.3 jit_solution(15145874251944954683)
XLA Ops:
  10.8 14.6 %all_gather.15 = bf16[3,768,192]{2,0,1:T(4,128)(2,1)S(1)} all-gather(bf16[3,96,192]{2,0,1:T(4,128)(2,1)S(1)} %copy.110), channel_id=1, replica_groups=mesh['dp'=8,'mp'=4] {'dp'}, dimensions={1}, use_global_device_ids=true | all-gather | bytes 995328 | tf_op jit(solution)/shard_map/all_gather | solution.py:55
  26.4 8.5 %all_gather.16 = bf16[192,768]{0,1:T(8,128)(2,1)S(1)} all-gather(bf16[192,96]{0,1:T(8,128)(2,1)S(1)} %copy.117), channel_id=1, replica_groups=mesh['dp'=8,'mp'=4] {'dp'}, dimensions={1}, use_global_device_ids=true | all-gather | bytes 331776 | tf_op jit(solution)/shard_map/all_gather | solution.py:56
  35.0 11.2 %all-gather.3.cloned.1.call-done = bf16[784,768]{0,1:T(8,128)(2,1)} async-done(((bf16[784,192]{0,1:T(8,128)(2,1)}), bf16[784,768]{0,1:T(8,128)(2,1)}) %all-gather.3.cloned.1.call-update) | async-done | bytes 1204240 | tf_op jit(solution)/shard_map/all_gather | solution.py:41
  46.1 1.7 copy.109
  48.7 1.3 fusion.50
  52.7 1.7 multiply_reduce_fusion.6
  56.6 2.1 reshape.118
  58.7 3.0 fusion.105
  61.7 18.8 %all-gather.5.cloned.1.call-done = bf16[784,768]{0,1:T(8,128)(2,1)} async-done(((bf16[784,192]{0,1:T(8,128)(2,1)}), bf16[784,768]{0,1:T(8,128)(2,1)}) %all-gather.5.cloned.1.call-update) | async-done | bytes 1204240 | tf_op jit(solution)/shard_map/all_gather | solution.py:42
  80.5 2.5 copy.125
  83.0 2.3 reshape.122
  85.3 94.5 %all-reduce.6.cloned.1.call-done = f32[784,768]{1,0:T(8,128)} async-done(((f32[784,768]{1,0:T(8,128)}), f32[784,768]{1,0:T(8,128)}) %all-reduce.6.cloned.1.call-update) | async-done | bytes 2408464 | tf_op jit(solution)/shard_map/psum | solution.py:78
  179.7 2.3 fusion.100
  184.8 2.2 reshape.120
  187.1 1.6 convolution_convert_fusion.3
  189.3 3.7 all-to-all-start.2
  193.3 1.6 convolution_convert_fusion.4
  195.7 2.5 all-to-all-done.2
  198.2 3.5 all-to-all-start
  202.4 1.5 all_to_all.63
  204.0 2.7 all-to-all-done
  207.4 3.0 fusion.19
  210.5 3.8 fusion.24
  214.3 3.4 fusion.59
  218.3 1.5 fusion.21
  219.8 25.1 %all-reduce.9 = (bf16[32,2,768]{2,0,1:T(8,128)(2,1)}, bf16[32,2,768]{2,0,1:T(8,128)(2,1)}) all-reduce(f32[32,2,768]{2,0,1:T(8,128)} %fusion.24, f32[32,2,768]{2,0,1:T(8,128)} %fusion.21), channel_id=1, replica_groups=mesh['dp'=8,'mp'=4] {'mp'}, use_global_device_ids=true, to_apply=%region_11.0 | all-reduce | flops 98304 | bytes 589824 | tf_op jit(solution)/shard_map/psum | solution.py:101
  244.8 1.6 copy.123
  246.5 4.0 all-to-all-start.1
  250.5 1.6 copy.129
  252.1 3.6 all-to-all-done.1
  255.7 4.0 all-to-all-start.3
  259.7 1.6 copy.220
  261.3 1.6 all_to_all.59
  262.9 1.8 convolution_bitcast_fusion.3
  265.3 1.6 copy.218
  266.9 1.6 all_to_all.67
  268.5 2.9 fusion.80
  271.4 3.2 fusion.35
  274.7 1.4 copy.131
  276.9 2.8 reshape.123
  279.7 4.4 multiply_reduce_fusion.1
  285.3 1.4 copy-done.4
  286.7 1.4 convolution_convert_fusion.2
  288.1 1.3 reshape.124
  289.4 1.3 fusion.10
  290.7 2.7 multiply_reduce_fusion
  293.5 1.6 convolution_bitcast_fusion.2
  295.7 2.3 multiply_convert_fusion
  302.8 3.8 convolution_bitcast_fusion
  306.7 1.2 copy-done.3
  308.0 2.5 convolution_bitcast_fusion.1
  310.5 2.7 copy.151
  313.2 4.8 reshape.129
  318.0 3.0 fusion.106
  321.1 3.1 fusion.94
  324.2 2.0 fusion.84
  326.2 3.0 reshape.121
  329.4 4.5 reduce-scatter.9.cloned.1.call-done
  334.0 1.6 copy.154
  335.6 98.1 %all-reduce.8.cloned.1.call-done = f32[784,768]{1,0:T(8,128)} async-done(((f32[784,768]{1,0:T(8,128)}), f32[784,768]{1,0:T(8,128)}) %all-reduce.8.cloned.1.call-update) | async-done | bytes 2408464 | tf_op jit(solution)/shard_map/psum | solution.py:195
  433.7 2.7 fusion.99
  436.4 3.4 dynamic-slice_add_fusion
  442.2 25.3 %all-reduce = (f32[768,16]{0,1:T(8,128)}, f32[4,768]{1,0:T(4,128)}) all-reduce(f32[768,16]{0,1:T(8,128)S(1)} %fusion.107, f32[4,768]{1,0:T(4,128)S(1)} %pad_maximum_fusion), channel_id=1, replica_groups=mesh['dp'=8,'mp'=4] {'dp'}, use_global_device_ids=true, to_apply=%region_23.0 | all-reduce | flops 15360 | bytes 122880 | tf_op jit(solution)/shard_map/psum | solution.py:210
  467.5 9.0 %reduce-scatter.7.cloned.1.call-done = f32[96,576]{1,0:T(8,128)} async-done(((f32[768,576]{1,0:T(8,128)}), f32[96,576]{1,0:T(8,128)}) %reduce-scatter.7.cloned.1.call-update) | async-done | bytes 221200
  (165 shorter events, 29.3 us)
Async XLA Ops:
  7.2 39.0 %all-gather.3.cloned.1.call-start = ((), (), s32[]{:S(2)}) async-start(), calls=%async_computation.6 | async-start | bytes 1720320 | tf_op jit(solution)/shard_map/all_gather | solution.py:41
  7.9 72.6 %all-gather.5.cloned.1.call-start = ((), (), s32[]{:S(2)}) async-start(), calls=%async_computation.8 | async-start | bytes 1720320 | tf_op jit(solution)/shard_map/all_gather | solution.py:42
  8.7 171.1 %all-reduce.6.cloned.1.call-start = ((), (), s32[]{:S(2)}) async-start(), calls=%async_computation.7 | async-start | bytes 4816896 | tf_op jit(solution)/shard_map/psum | solution.py:78
  9.6 39.1 %copy-start.37 = (f32[768]{0:T(1024)}, f32[768]{0:T(1024)S(1)}, u32[]{:S(2)}) copy-start(f32[768]{0:T(1024)S(1)} %get-tuple-element.52) | copy-start | bytes 9220
  9.6 39.1 %copy-start.41 = (f32[768]{0:T(1024)}, f32[768]{0:T(1024)S(1)}, u32[]{:S(2)}) copy-start(f32[768]{0:T(1024)S(1)} %get-tuple-element.51) | copy-start | bytes 9220
  9.6 172.9 %copy-start.25 = (f32[768]{0:T(1024)}, f32[768]{0:T(1024)S(1)}, u32[]{:S(2)}) copy-start(f32[768]{0:T(1024)S(1)} %get-tuple-element.50) | copy-start | bytes 9220
  9.6 16.7 %copy-start.24 = (f32[192,96]{1,0:T(8,128)S(1)}, f32[192,96]{1,0:T(8,128)}, u32[]{:S(2)}) copy-start(f32[192,96]{1,0:T(8,128)} %param.11) | copy-start | bytes 221188
  26.3 22.4 %copy-start.16 = (bf16[3,768,192]{1,2,0:T(8,128)(2,1)}, bf16[3,768,192]{1,2,0:T(8,128)(2,1)S(1)}, u32[]{:S(2)}) copy-start(bf16[3,768,192]{1,2,0:T(8,128)(2,1)S(1)} %copy.111) | copy-start | bytes 2654212
  47.9 2.1 copy-start.2
  48.1 1.9 copy-start.31
  48.7 1.4 copy-start.29
  182.1 1.4 copy-start
  182.5 1.0 copy-start.22
  182.6 1.4 copy-start.27
  183.5 1.1 copy-start.6
  184.8 79.9 %copy-start.33 = (f32[4,196]{1,0:T(4,128)}, f32[4,196]{1,0:T(4,128)S(1)}, u32[]{:S(2)}) copy-start(f32[4,196]{1,0:T(4,128)S(1)} %sub.113) | copy-start | bytes 9412
  187.1 77.6 %copy-start.35 = (f32[4,196]{1,0:T(4,128)}, f32[4,196]{1,0:T(4,128)S(1)}, u32[]{:S(2)}) copy-start(f32[4,196]{1,0:T(4,128)S(1)} %div.46) | copy-start | bytes 9412
  189.3 8.8 %all-to-all-start.2 = ((bf16[4,16,768]{2,0,1:T(4,128)(2,1)}), bf16[4,16,768]{2,0,1:T(4,128)(2,1)S(1)}, u32[]{:S(2)}, u32[]{:S(2)}) async-start(bf16[4,16,768]{2,0,1:T(4,128)(2,1)} %copy.127), calls=%async_computation.2 | async-start | bytes 196608 | tf_op jit(solution)/shard_map/all_to_all | solution.py:115
  198.2 8.5 %all-to-all-start = ((bf16[4,16,768]{2,0,1:T(4,128)(2,1)}), bf16[4,16,768]{2,0,1:T(4,128)(2,1)S(1)}, u32[]{:S(2)}, u32[]{:S(2)}) async-start(bf16[4,16,768]{2,0,1:T(4,128)(2,1)} %copy.121), calls=%async_computation | async-start | bytes 196608 | tf_op jit(solution)/shard_map/all_to_all | solution.py:95
  207.4 10.9 %slice-start = ((s8[4718592]{0:T(1024)(128)(4,1)}), s8[4194304]{0:T(1024)(128)(4,1)S(1)}, s32[]{:S(2)}) async-start(s8[4718592]{0:T(1024)(128)(4,1)} %bitcast.187), calls=%async_computation.12 | async-start | bytes 8388608
  210.4 3.8 copy-start.17
  210.4 7.8 %slice-start.1 = ((s8[4718592]{0:T(1024)(128)(4,1)}), s8[524288]{0:T(1024)(128)(4,1)S(1)}, s32[]{:S(2)}) async-start(s8[4718592]{0:T(1024)(128)(4,1)} %bitcast.187), calls=%async_computation.13 | async-start | bytes 1048576
  217.6 0.6 copy-start.20
  246.5 9.2 %all-to-all-start.1 = ((bf16[32,2,768]{2,1,0:T(2,128)(2,1)}), bf16[32,2,768]{2,1,0:T(2,128)(2,1)}, u32[]{:S(2)}, u32[]{:S(2)}) async-start(bf16[32,2,768]{2,1,0:T(2,128)(2,1)} %copy.123), calls=%async_computation.1 | async-start | bytes 196608 | tf_op jit(solution)/shard_map/all_to_all | solution.py:102
  255.7 9.7 %all-to-all-start.3 = ((bf16[32,2,768]{2,1,0:T(2,128)(2,1)}), bf16[32,2,768]{2,1,0:T(2,128)(2,1)}, u32[]{:S(2)}, u32[]{:S(2)}) async-start(bf16[32,2,768]{2,1,0:T(2,128)(2,1)} %copy.129), calls=%async_computation.3 | async-start | bytes 196608 | tf_op jit(solution)/shard_map/all_to_all | solution.py:131
  259.7 74.3 %reduce-scatter.9.cloned.1.call-start = ((), (), s32[]{:S(2)}) async-start(), calls=%async_computation.11 | async-start | bytes 884736
  279.7 4.5 copy-start.1
  279.7 4.5 copy-start.10
  279.7 4.5 copy-start.26
  279.7 4.5 copy-start.28
  285.3 1.4 copy-start.4
  290.7 2.7 copy-start.5
  290.7 2.7 copy-start.13
  293.5 1.6 copy-start.14
  295.6 3.3 copy-start.12
  297.9 1.0 copy-start.8
  299.0 1.4 copy-start.11
  299.5 1.3 copy-start.9
  300.1 133.5 %all-reduce.8.cloned.1.call-start = ((), (), s32[]{:S(2)}) async-start(), calls=%async_computation.9 | async-start | bytes 4816896 | tf_op jit(solution)/shard_map/psum | solution.py:195
  301.9 1.0 copy-start.23
  306.6 1.3 copy-start.3
  306.6 1.3 copy-start.30
  306.7 1.3 copy-start.32
  306.7 1.3 copy-start.38
  306.7 1.3 copy-start.42
  306.7 169.8 %reduce-scatter.7.cloned.1.call-start = ((), (), s32[]{:S(2)}) async-start(), calls=%async_computation.10 | async-start | bytes 2211840
  313.2 4.8 copy-start.19
  313.2 4.8 copy-start.21
  318.0 3.0 copy-start.18
  321.0 3.1 copy-start.40
  321.0 3.1 copy-start.39
  321.0 3.1 copy-start.15
  321.0 3.1 copy-start.34
  321.1 3.1 copy-start.36
  326.2 3.0 copy-start.7
Sparse Core Ops, SparseCore 0:
  9.6 36.5 all-gather.2
  47.7 32.7 all-gather.4
  83.4 96.2 all-reduce.5
  300.2 33.6 reduce-scatter.8
  336.3 97.2 all-reduce.7
  436.9 39.5 reduce-scatter.6
where the time goes:
time: 487 us; the launch traced here: 485 us
  waiting for transfers between devices  246 us (51%)
  blocking collectives  73.6 us (15%)
  local copies, waits for them, and re-layouts  62.1 us (13%)
  matrix products  56.7 us (12%)
  other arithmetic  16.1 us (3%)
  starting transfers between devices  15.6 us (3%)
  between operations  14.8 us (3%)
    psum x1, waiting for transfers between devices, per_device(): grad_first = lax.psum(first_grad_part, 'mp')  98.1 us
    psum x1, waiting for transfers between devices, per_device(): branch = lax.psum(branch_part, 'mp')  94.5 us
    psum x1, blocking collectives, per_device(): phi_grad, norm_grad = lax.psum((phi_part, norm_part), 'dp')  25.3 us
    psum x1, blocking collectives, per_device(): results = lax.psum(result_part, 'mp').astype(jnp.bfloat16)  25.1 us
    unnamed x100, local copies, waits for them, and re-layouts  20.3 us
    all_gather x1, waiting for transfers between devices, per_device(): lax.all_gather(cotangent, 'mp', axis=1, tiled=True)  18.8 us
    unnamed x8, waiting for transfers between devices  15 us
    all_gather x1, blocking collectives, per_device(): lax.all_gather(qkv_local, 'dp', axis=1, tiled=True)  14.6 us
  transfers between devices with their start and end apart: 10, of which 9 were waited for; matrix products, arithmetic and copies ran while one was open for 14% of the time, Pallas kernels for 0%

commit v1 on v0

v1 whole, which is shorter than its diff:
```python
import functools
import math

import jax
import jax.numpy as jnp
from jax import lax
from jax.experimental import pallas as pl
from jax.experimental.pallas import tpu as pltpu
from jax.sharding import PartitionSpec as P

HEAD_DIM = 64
SEQ = 196
EPSILON = 1e-06
MESH = pl.DeviceIdType.MESH
BF = jnp.bfloat16
F32 = jnp.float32
NEG = -1e30


def nn(a, b):
    return lax.dot_general(a, b, (((1,), (0,)), ((), ())), preferred_element_type=F32)


def nt(a, b):
    return lax.dot_general(a, b, (((1,), (1,)), ((), ())), preferred_element_type=F32)


def tn(a, b):
    return lax.dot_general(a, b, (((0,), (0,)), ((), ())), preferred_element_type=F32)


def each(low, high, body):
    if high - low <= 8:
        for i in range(low, high):
            body(i)
    else:

        def step(i, carry):
            body(i)
            return carry

        lax.fori_loop(low, high, step, 0)


def select_rows(rows, cols, source):
    row = lax.broadcasted_iota(jnp.int32, (rows, cols), 0)
    col = lax.broadcasted_iota(jnp.int32, (rows, cols), 1)
    return jnp.where(col == source(row), 1.0, 0.0).astype(BF)


def normalize(values):
    mean = jnp.mean(values, axis=-1, keepdims=True)
    centered = values - mean
    var = jnp.mean(centered * centered, axis=-1, keepdims=True)
    inv = lax.rsqrt(var + EPSILON)
    return centered * inv, inv


def norm_backward(grad, gain, normed, inv):
    scaled = grad * gain
    first = jnp.mean(scaled, axis=-1, keepdims=True)
    second = jnp.mean(scaled * normed, axis=-1, keepdims=True)
    return inv * (scaled - first - normed * second)


class Sizes:
    def __init__(self, mesh, tokens, w_qkv, phi, w_in):
        self.DP, self.MP = mesh.shape["dp"], mesh.shape["mp"]
        self.D, self.E = phi.shape
        self.CW = tokens.shape[1]
        self.RB = w_qkv.shape[1]
        self.QW = 3 * self.CW
        self.HL = self.CW // HEAD_DIM
        self.EPD = w_in.shape[0]
        self.F = w_in.shape[2]
        self.IN = 2 if self.DP % 2 == 0 else 1
        self.NX = self.DP // self.IN
        self.SP = (SEQ + 15) // 16 * 16
        self.ROWS = tokens.shape[0]
        self.TR = (2 * self.EPD + 7) // 8 * 8
        self.SUM = self.E + 8
        self.own_weights = self.RB % 16 == 0 and self.DP <= 8


def scratch_of(z):
    dma = pltpu.SemaphoreType.DMA
    v = pltpu.VMEM
    DP, MP, D, CW, RB, QW, SP, NX, IN = z.DP, z.MP, z.D, z.CW, z.RB, z.QW, z.SP, z.NX, z.IN
    items = dict(
        tsend=v((MP, SP, CW), BF), tin=v((MP, SP, CW), BF),
        csend=v((MP, SP, CW), BF), cin=v((MP, SP, CW), BF),
        osend=v((MP, SP, CW), BF), oin=v((MP, SP, CW), BF),
        isend=v((MP, SP, CW), BF), iin=v((MP, SP, CW), BF),
        wf_in=v((z.EPD, D, z.F), F32), wf_out=v((z.EPD, z.F, D), F32),
        wb_in=v((z.EPD, D, z.F), BF), wb_out=v((z.EPD, z.F, D), BF),
        h1=v((SP, D), BF), qkv=v((MP, SP, QW), BF), probs=v((MP, z.HL, SP, SP), F32),
        att=v((MP, SP, CW), BF), dqkv=v((SP, QW), BF), datt=v((MP, SP, CW), BF),
        resid=v((SP, D), F32), dresid=v((SP, D), F32), dh1=v((SP, D), F32),
        slot_out=v((DP * z.TR, D), F32), slot_in=v((DP * z.TR, D), F32),
        slot_all=v((MP, 2 * z.EPD * DP, D), BF),
        part=v((MP, 2 * z.EPD * DP, D), F32), psend=v((MP, 2 * z.EPD * DP, D), BF),
        pin=v((MP, 2 * z.EPD * DP, D), BF),
        back_out=v((DP * z.TR, D), F32), back_in=v((DP * z.TR, D), F32),
    )
    sems = dict(
        tok=(2, MP), cot=(2, MP), outs=(2, MP), ings=(2, MP), hbm=(2,),
        dp1=(2, DP), mp1=(2, MP), mp2=(2, MP), dp2=(2, DP),
    )
    if z.own_weights:
        items.update(
            wall=v((MP, NX, IN, RB, QW), BF), wpall=v((MP, NX, IN, RB, CW), BF),
            gq=v((MP, NX, IN, RB, QW), BF), gp=v((MP, NX, IN, RB, CW), BF),
            cq=v((MP, NX, RB, QW), BF), cp=v((MP, NX, RB, CW), BF),
            xq=v((MP, NX, RB, QW), BF), xp=v((NX, MP, RB, CW), BF),
            yq=v((MP, NX, RB, QW), BF), yp=v((NX, MP, RB, CW), BF),
            zq=v((MP, RB, QW), BF), zp=v((MP, RB, CW), BF),
            rq=v((MP, RB, QW), BF), rp=v((MP, RB, CW), BF),
            sums_p=v((MP, RB, CW), F32),
            sa=v((z.SUM, D), F32), sb=v((IN, z.SUM, D), F32), sc=v((NX, z.SUM, D), F32),
            sd=v((MP, z.SUM, D), F32),
            ta=v((8, D), F32), tb=v((IN, 8, D), F32), tc=v((NX, 8, D), F32), td=v((MP, 8, D), F32),
        )
        sems.update(
            wz=(2, MP), wx=(2, MP, NX), wc=(2, MP), vz=(2, MP), vx=(2, NX), vc=(2,),
            gc=(2, MP), gx=(2, MP, NX), gz=(2, MP), hc=(2,), hx=(2, NX), hz=(2, MP),
            s1=(2,), s2=(2, NX), s3=(2, MP), t1=(2,), t2=(2, NX), t3=(2, MP),
        )
    names, shapes = [], []
    for name, shape in items.items():
        names.append(name)
        shapes.append(shape)
    for name, shape in sems.items():
        names.append("m_" + name)
        shapes.append(dma(shape))
    return names, shapes


class Refs:
    pass


def block_kernel(z, in_names, out_names, names, *refs):
    r = Refs()
    for name, ref in zip(in_names + out_names + names, refs):
        setattr(r, name, ref)
    DP, MP, D, CW, RB, QW, SP = z.DP, z.MP, z.D, z.CW, z.RB, z.QW, z.SP
    NX, IN, E, EPD, TR = z.NX, z.IN, z.E, z.EPD, z.TR
    KE = 2 * EPD
    dp, mp = lax.axis_index("dp"), lax.axis_index("mp")
    xy, co = dp // IN, lax.rem(dp, IN)
    sends = []

    def remote(src, dst, sem, s_at, r_at, device):
        return pltpu.make_async_remote_copy(
            src_ref=src, dst_ref=dst, send_sem=sem.at[(0,) + s_at], recv_sem=sem.at[(1,) + r_at],
            device_id=device, device_id_type=MESH,
        )

    def mp_at(k):
        return lax.rem(mp + k, MP)

    def dp_at(k):
        return lax.rem(dp + k, DP)

    def xy_at(k):
        return lax.rem(xy + k, NX)

    def to_mp(k):
        return (dp, mp_at(k))

    def to_xy(k):
        return (xy_at(k) * IN + co, mp)

    def to_core():
        return (xy * IN + 1 - co, mp)

    barrier = pltpu.get_barrier_semaphore()
    for k in range(1, MP):
        pl.semaphore_signal(barrier, inc=1, device_id=to_mp(k), device_id_type=MESH)
    each(1, DP, lambda k: pl.semaphore_signal(barrier, inc=1, device_id=(dp_at(k), mp), device_id_type=MESH))

    load_in = pltpu.make_async_copy(r.w_in, r.wf_in, r.m_hbm.at[0])
    load_out = pltpu.make_async_copy(r.w_out, r.wf_out, r.m_hbm.at[1])
    load_in.start()
    load_out.start()

    if z.own_weights:
        r.wall[mp, xy, co] = jnp.concatenate([r.w_qkv[c].astype(BF) for c in range(3)], axis=1)
        r.wpall[mp, xy, co] = r.w_proj[...].T.astype(BF)

    def to_images(source, target):
        target[...] = jnp.zeros((MP, SP, CW), BF)
        for i in range(MP):
            target[i, 0:SEQ, :] = source[pl.ds(SEQ * i, SEQ), :]

    to_images(r.tokens, r.tsend)
    pl.semaphore_wait(barrier, MP - 1 + DP - 1)

    def swap(src, dst, sem, k):
        return remote(src.at[mp_at(k)], dst.at[mp], sem, (k,), (MP - k,), to_mp(k))

    def swap_start(src, dst, sem):
        for k in range(1, MP):
            swap(src, dst, sem, k).start()
        dst[mp] = src[mp]
        sends.extend((lambda k=k: swap(src, dst, sem, k).wait_send()) for k in range(1, MP))

    def swap_wait(src, dst, sem):
        for k in range(1, MP):
            remote(src.at[mp_at(k)], dst.at[mp_at(k)], sem, (k,), (k,), to_mp(k)).wait_recv()

    def wz(k):
        block = r.wall.at[mp, xy, co]
        return remote(block, block, r.m_wz, (k,), (MP - k,), to_mp(k))

    def wz_wait(k):
        block = r.wall.at[mp_at(k), xy, co]
        remote(block, block, r.m_wz, (k,), (k,), to_mp(k)).wait_recv()

    def wx(j, k):
        block = r.wall.at[mp_at(j), xy, co]
        return remote(block, block, r.m_wx, (j, k), (j, NX - k), to_xy(k))

    def wx_wait(j, k):
        block = r.wall.at[mp_at(j), xy_at(k), co]
        remote(block, block, r.m_wx, (j, k), (j, k), to_xy(k)).wait_recv()

    def wc(j):
        block = r.wall.at[mp_at(j), :, co]
        return remote(block, block, r.m_wc, (j,), (j,), to_core())

    def wc_wait(j):
        block = r.wall.at[mp_at(j), :, 1 - co]
        remote(block, block, r.m_wc, (j,), (j,), to_core()).wait_recv()

    def vz(k):
        block = r.wpall.at[mp, xy, co]
        return remote(block, block, r.m_vz, (k,), (MP - k,), to_mp(k))

    def vz_wait(k):
        block = r.wpall.at[mp_at(k), xy, co]
        remote(block, block, r.m_vz, (k,), (k,), to_mp(k)).wait_recv()

    def vx(k):
        block = r.wpall.at[:, xy, co]
        return remote(block, block, r.m_vx, (k,), (NX - k,), to_xy(k))

    def vx_wait(k):
        block = r.wpall.at[:, xy_at(k), co]
        remote(block, block, r.m_vx, (k,), (k,), to_xy(k)).wait_recv()

    def vc():
        block = r.wpall.at[:, :, co]
        return remote(block, block, r.m_vc, (), (), to_core())

    def vc_wait():
        block = r.wpall.at[:, :, 1 - co]
        remote(block, block, r.m_vc, (), (), to_core()).wait_recv()

    if z.own_weights:
        for k in range(1, MP):
            wz(k).start()
        for k in range(1, NX):
            wx(0, k).start()
    swap_start(r.tsend, r.tin, r.m_tok)
    if z.own_weights:
        for k in range(1, MP):
            vz(k).start()
    to_images(r.cotangent, r.csend)
    swap_start(r.csend, r.cin, r.m_cot)

    load_in.wait()
    r.wb_in[...] = r.wf_in[...].astype(BF)
    if z.own_weights:
        for j in range(1, MP):
            wz_wait(j)
            for k in range(1, NX):
                wx(j, k).start()
    load_out.wait()
    r.wb_out[...] = r.wf_out[...].astype(BF)

    swap_wait(r.tsend, r.tin, r.m_tok)
    gain1, shift1 = r.norm_params[0:1, :], r.norm_params[1:2, :]
    gain2, shift2 = r.norm_params[2:3, :], r.norm_params[3:4, :]

    def own_image(ref):
        return jnp.concatenate([ref[i] for i in range(MP)], axis=1).astype(F32)

    normed1, _ = normalize(own_image(r.tin))
    r.h1[...] = (normed1 * gain1 + shift1).astype(BF)

    scale = 1.0 / math.sqrt(HEAD_DIM)
    key_ok = lax.broadcasted_iota(jnp.int32, (1, SP), 1) < SEQ

    def weight(m):
        return r.wall[m].reshape(D, QW) if z.own_weights else r.wall[m]

    def proj_weight(m):
        return r.wpall[m].reshape(D, CW) if z.own_weights else r.wpall[m]

    if z.own_weights:
        for k in range(1, NX):
            wx_wait(0, k)
        wc(0).start()
        wc_wait(0)

    def heads_forward(j, carry):
        m = mp_at(j)
        qkv = nn(r.h1[...], weight(m)).astype(BF)
        r.qkv[m] = qkv
        if z.own_weights:

            @pl.when(j < MP - 1)
            def _():
                for k in range(1, NX):
                    wx_wait(j + 1, k)
                wc(j + 1).start()

            @pl.when(j == 0)
            def _():
                for k in range(1, MP):
                    vz_wait(k)
                for k in range(1, NX):
                    vx(k).start()

            @pl.when(j == MP - 1)
            def _():
                for k in range(1, NX):
                    vx_wait(k)
                vc().start()

        attended = []
        for h in range(z.HL):
            query, key, value = (
                qkv[:, c * CW + h * HEAD_DIM : c * CW + (h + 1) * HEAD_DIM] for c in range(3)
            )
            scores = jnp.where(key_ok, nt(query, key) * scale, NEG)
            top = jnp.max(scores, axis=-1, keepdims=True)
            grown = jnp.exp(scores - top)
            probs = grown / jnp.sum(grown, axis=-1, keepdims=True)
            r.probs[m, h] = probs
            attended.append(nn(probs.astype(BF), value))
        r.att[m] = jnp.concatenate(attended, axis=1).astype(BF)
        if z.own_weights:

            @pl.when(j < MP - 1)
            def _():
                wc_wait(j + 1)

        return carry

    lax.fori_loop(0, MP, heads_forward, 0)
    if z.own_weights:
        vc_wait()

    resid = own_image(r.tin)
    for m in range(MP):
        resid = resid + nt(r.att[m], proj_weight(m))
    r.resid[...] = resid
    normed2, inv2 = normalize(resid)
    h2 = (normed2 * gain2 + shift2).astype(BF)
    phi_low = r.phi[...].astype(BF)
    logits = nn(h2, phi_low)
    token_ok = lax.broadcasted_iota(jnp.int32, (SP, 1), 0) < SEQ
    masked = jnp.where(token_ok, logits, NEG)
    grown = jnp.exp(masked - jnp.max(masked, axis=0, keepdims=True))
    dispatch = grown / jnp.sum(grown, axis=0, keepdims=True)
    grown = jnp.exp(logits - jnp.max(logits, axis=1, keepdims=True))
    combine = grown / jnp.sum(grown, axis=1, keepdims=True)
    dispatch_low, combine_low = dispatch.astype(BF), combine.astype(BF)
    swap_wait(r.csend, r.cin, r.m_cot)
    grad = jnp.concatenate([r.cin[i] for i in range(MP)], axis=1)
    slots = tn(dispatch_low, h2).astype(BF)
    dresults = tn(combine_low, grad).astype(BF)

    def out_row(row):
        d, q = row // TR, row % TR
        return jnp.where(q < KE, (q // EPD) * E + d * EPD + q % EPD, -1)

    r.slot_out[...] = nn(select_rows(DP * TR, 2 * E, out_row), jnp.concatenate([slots, dresults], axis=0))

    def rows_of(ref, d):
        return ref.at[pl.ds(pl.multiple_of(d * TR, 8), TR)]

    def dp_swap(src, dst, sem):
        def copy(k):
            return remote(rows_of(src, dp_at(k)), rows_of(dst, dp), sem, (k,), (DP - k,), (dp_at(k), mp))

        each(1, DP, lambda k: copy(k).start())
        here = pl.ds(pl.multiple_of(dp * TR, 8), TR)
        dst[here, :] = src[here, :]
        sends.append(lambda: each(1, DP, lambda k: copy(k).wait_send()))

        def arrive(k):
            remote(rows_of(src, dp_at(k)), rows_of(dst, dp_at(k)), sem, (k,), (k,), (dp_at(k), mp)).wait_recv()

        each(1, DP, arrive)

    dp_swap(r.slot_out, r.slot_in, r.m_dp1)
    gather_rows = select_rows(KE * DP, DP * TR, lambda row: (row % DP) * TR + row // DP)
    r.slot_all[mp] = nn(gather_rows, r.slot_in[...].astype(BF)).astype(BF)

    def slot_copy(k):
        return remote(r.slot_all.at[mp], r.slot_all.at[mp], r.m_mp1, (k,), (MP - k,), to_mp(k))

    for k in range(1, MP):
        slot_copy(k).start()
        sends.append(lambda k=k: slot_copy(k).wait_send())
    for k in range(1, MP):
        block = r.slot_all.at[mp_at(k)]
        remote(block, block, r.m_mp1, (k,), (k,), to_mp(k)).wait_recv()

    everything = [r.slot_all[m].astype(F32) for m in range(MP)]

    def expert_rows(q):
        return jnp.concatenate([one[q * DP : (q + 1) * DP] for one in everything], axis=0).astype(BF)

    for e in range(EPD):
        slots_e, dresults_e = expert_rows(e), expert_rows(EPD + e)
        pre = nn(slots_e, r.wb_in[e])
        cdf = 0.5 * (1.0 + lax.erf(pre * (1.0 / math.sqrt(2.0))))
        hidden = (pre * cdf).astype(BF)
        results_e = nn(hidden, r.wb_out[e])
        slope = cdf + pre * jnp.exp(-0.5 * pre * pre) * (1.0 / math.sqrt(2.0 * math.pi))
        dpre = (nt(dresults_e, r.wb_out[e]) * slope).astype(BF)
        dslots_e = nt(dpre, r.wb_in[e])
        r.slots[e], r.dresults[e], r.hidden[e], r.dpre[e] = slots_e, dresults_e, hidden, dpre
        for m in range(MP):
            r.part[m, e * DP : (e + 1) * DP, :] = results_e[m * DP : (m + 1) * DP]
            r.part[m, (EPD + e) * DP : (EPD + e + 1) * DP, :] = dslots_e[m * DP : (m + 1) * DP]

    r.psend[...] = r.part[...].astype(BF)

    def part_copy(k):
        return remote(r.psend.at[mp_at(k)], r.pin.at[MP - k], r.m_mp2, (k,), (MP - k,), to_mp(k))

    for k in range(1, MP):
        part_copy(k).start()
        sends.append(lambda k=k: part_copy(k).wait_send())
    total = r.part[mp]
    for k in range(1, MP):
        remote(r.psend.at[mp_at(k)], r.pin.at[k], r.m_mp2, (k,), (k,), to_mp(k)).wait_recv()
        total = total + r.pin[k].astype(F32)

    def back_row(row):
        d, q = row // TR, row % TR
        return jnp.where(q < KE, q * DP + d, -1)

    r.back_out[...] = nn(select_rows(DP * TR, KE * DP, back_row), total.astype(BF))
    dp_swap(r.back_out, r.back_in, r.m_dp2)

    def result_row(row):
        kind, e = row // E, row % E
        return (e // EPD) * TR + kind * EPD + e % EPD

    both = nn(select_rows(2 * E, DP * TR, result_row), r.back_in[...].astype(BF)).astype(BF)
    results, dslots = both[:E], both[E:]

    output = r.resid[...] + nn(combine_low, results)
    for m in range(MP):
        r.osend[m] = output[:, m * CW : (m + 1) * CW].astype(BF)
    swap_start(r.osend, r.oin, r.m_outs)
    dcombine, ddispatch = nt(grad, results), nt(h2, dslots)
    dlogits = dispatch * (ddispatch - jnp.sum(dispatch * ddispatch, axis=0, keepdims=True))
    dlogits = dlogits + combine * (dcombine - jnp.sum(combine * dcombine, axis=1, keepdims=True))
    dlogits = dlogits.astype(BF)
    dh2 = nn(dispatch_low, dslots) + nt(dlogits, phi_low)
    gain_part2 = jnp.sum(dh2 * normed2, axis=0, keepdims=True)
    shift_part2 = jnp.sum(dh2, axis=0, keepdims=True)
    dresid = grad.astype(F32) + norm_backward(dh2, gain2, normed2, inv2)
    r.dresid[...] = dresid
    dbranch = dresid.astype(BF)
    for m in range(MP):
        r.datt[m] = nn(dbranch, proj_weight(m)).astype(BF)
        piece = tn(dbranch, r.att[m])
        if z.own_weights:
            r.gp[m] = piece.astype(BF).reshape(NX, IN, RB, CW)
        else:
            r.gp[m] = piece.astype(BF)

    def hc():
        return remote(r.gp.at[:, :, 1 - co], r.cp, r.m_hc, (), (), to_core())

    def hx(k):
        return remote(r.xp.at[xy_at(k)], r.yp.at[NX - k], r.m_hx, (k,), (NX - k,), to_xy(k))

    def hz(k):
        return remote(r.zp.at[k], r.rp.at[MP - k], r.m_hz, (k,), (MP - k,), to_mp(k))

    def gc(j):
        return remote(r.gq.at[mp_at(j), :, 1 - co], r.cq.at[j], r.m_gc, (j,), (j,), to_core())

    def gx(j, k):
        return remote(r.xq.at[j, xy_at(k)], r.yq.at[j, NX - k], r.m_gx, (j, k), (j, NX - k), to_xy(k))

    def gz(k):
        return remote(r.zq.at[k], r.rq.at[MP - k], r.m_gz, (k,), (MP - k,), to_mp(k))

    def hc_finish():
        hc().wait_recv()
        for x in range(NX):
            r.xp[x] = (r.gp[:, x, co].astype(F32) + r.cp[:, x].astype(F32)).astype(BF)
        for k in range(1, NX):
            hx(k).start()

    def gc_finish(j):
        gc(j).wait_recv()
        m = mp_at(j)
        for x in range(NX):
            r.xq[j, x] = (r.gq[m, x, co].astype(F32) + r.cq[j, x].astype(F32)).astype(BF)
        for k in range(1, NX):
            gx(j, k).start()

    def gx_total(j):
        total = r.xq[j, xy].astype(F32)
        for k in range(1, NX):
            remote(r.xq.at[j, xy_at(k)], r.yq.at[j, k], r.m_gx, (j, k), (j, k), to_xy(k)).wait_recv()
            total = total + r.yq[j, k].astype(F32)
        return total

    def gx_finish(j):
        r.zq[j] = gx_total(j).astype(BF)
        gz(j).start()

    def small_core(a, b, sem):
        copy = remote(a, b.at[co], sem, (), (), to_core())
        copy.start()
        b[co] = a[...]
        sends.append(copy.wait_send)

    def small_core_finish(a, b, c, sem1, sem2):
        remote(a, b.at[1 - co], sem1, (), (), to_core()).wait_recv()
        c[xy] = sum_of(b, IN)
        for k in range(1, NX):
            copy = remote(c.at[xy], c.at[xy], sem2, (k,), (NX - k,), to_xy(k))
            copy.start()
            sends.append(copy.wait_send)

    def small_plane_finish(c, d, sem2, sem3):
        for k in range(1, NX):
            block = c.at[xy_at(k)]
            remote(block, block, sem2, (k,), (k,), to_xy(k)).wait_recv()
        d[mp] = sum_of(c, NX)
        for k in range(1, MP):
            copy = remote(d.at[mp], d.at[mp], sem3, (k,), (MP - k,), to_mp(k))
            copy.start()
            sends.append(copy.wait_send)

    def small_finish(d, sem3):
        for k in range(1, MP):
            block = d.at[mp_at(k)]
            remote(block, block, sem3, (k,), (k,), to_mp(k)).wait_recv()
        return sum_of(d, MP)

    def sum_of(ref, count):
        total = ref[0]
        for i in range(1, count):
            total = total + ref[i]
        return total

    pad = jnp.zeros((6, D), F32)
    rows2 = jnp.concatenate([gain_part2, shift_part2, pad], axis=0)
    phi_to = r.sa if z.own_weights else r.phi_grad
    phi_to[0:E, :] = tn(dlogits, h2)
    if z.own_weights:
        hc().start()
        r.sa[E : E + 8, :] = rows2
        small_core(r.sa, r.sb, r.m_s1)
        hc_finish()
        small_core_finish(r.sa, r.sb, r.sc, r.m_s1, r.m_s2)

    r.dh1[...] = jnp.zeros((SP, D), F32)

    def heads_backward(i, carry):
        j = lax.rem(i + 1, MP)
        m = mp_at(j)
        qkv, datt = r.qkv[m], r.datt[m]
        pieces = [[], [], []]
        for h in range(z.HL):
            query, key, value = (
                qkv[:, c * CW + h * HEAD_DIM : c * CW + (h + 1) * HEAD_DIM] for c in range(3)
            )
            grad_h = datt[:, h * HEAD_DIM : (h + 1) * HEAD_DIM]
            probs = r.probs[m, h]
            dprobs = nt(grad_h, value)
            dscores = probs * (dprobs - jnp.sum(probs * dprobs, axis=-1, keepdims=True))
            dscores = dscores.astype(BF)
            pieces[0].append(nn(dscores, key) * scale)
            pieces[1].append(tn(dscores, query) * scale)
            pieces[2].append(tn(probs.astype(BF), grad_h))
        dqkv = jnp.concatenate(pieces[0] + pieces[1] + pieces[2], axis=1).astype(BF)
        piece = tn(r.h1[...], dqkv)
        if z.own_weights:
            r.gq[m] = piece.astype(BF).reshape(NX, IN, RB, QW)
            gc(j).start()
        else:
            r.gq[m] = piece.astype(BF)
        r.dh1[...] += nt(dqkv, weight(m))
        if z.own_weights:

            @pl.when(i >= 1)
            def _():
                gc_finish(i)

            @pl.when(i >= 2)
            def _():
                gx_finish(i - 1)

        return carry

    lax.fori_loop(0, MP, heads_backward, 0)

    normed1, inv1 = normalize(own_image(r.tin))
    dh1 = r.dh1[...]
    gain_part1 = jnp.sum(dh1 * normed1, axis=0, keepdims=True)
    shift_part1 = jnp.sum(dh1, axis=0, keepdims=True)
    late = jnp.concatenate([gain_part1, shift_part1, pad], axis=0)
    if z.own_weights:
        gc_finish(0)
        r.ta[...] = late
        small_core(r.ta, r.tb, r.m_t1)
    input_grad = r.dresid[...] + norm_backward(dh1, gain1, normed1, inv1)
    for m in range(MP):
        r.isend[m] = input_grad[:, m * CW : (m + 1) * CW].astype(BF)
    swap_start(r.isend, r.iin, r.m_ings)

    if z.own_weights:
        gx_finish(MP - 1)
        small_core_finish(r.ta, r.tb, r.tc, r.m_t1, r.m_t2)
        total = r.xp[xy].astype(F32)
        for k in range(1, NX):
            remote(r.xp.at[xy_at(k)], r.yp.at[k], r.m_hx, (k,), (k,), to_xy(k)).wait_recv()
            total = total + r.yp[k].astype(F32)
        r.sums_p[...] = total
        for k in range(1, MP):
            r.zp[k] = r.sums_p[mp_at(k)].astype(BF)
            hz(k).start()
        small_plane_finish(r.sc, r.sd, r.m_s2, r.m_s3)
        own = gx_total(0)
        small_plane_finish(r.tc, r.td, r.m_t2, r.m_t3)

    def from_images(source, target):
        for i in range(MP):
            target[pl.ds(SEQ * i, SEQ), :] = source[i, 0:SEQ, :].astype(F32)

    swap_wait(r.osend, r.oin, r.m_outs)
    from_images(r.oin, r.output)
    if z.own_weights:
        total = r.sums_p[mp]
        for k in range(1, MP):
            remote(r.zp.at[k], r.rp.at[k], r.m_hz, (k,), (k,), to_mp(k)).wait_recv()
            total = total + r.rp[k].astype(F32)
        r.proj_grad[...] = total.T
        for k in range(1, MP):
            remote(r.zq.at[k], r.rq.at[k], r.m_gz, (k,), (k,), to_mp(k)).wait_recv()
            own = own + r.rq[k].astype(F32)
        for c in range(3):
            r.qkv_grad[c] = own[:, c * CW : (c + 1) * CW]
        first = small_finish(r.sd, r.m_s3)
        second = small_finish(r.td, r.m_t3)
        r.phi_grad[...] = first[:E]
        r.norm_grad[...] = jnp.concatenate([second[0:2], first[E : E + 2]], axis=0)
    else:
        r.norm_grad[...] = jnp.concatenate([late[0:2], rows2[0:2]], axis=0)
    swap_wait(r.isend, r.iin, r.m_ings)
    from_images(r.iin, r.input_grad)

    if z.own_weights:
        for k in range(1, MP):
            wz(k).wait_send()
            vz(k).wait_send()
            gz(k).wait_send()
            hz(k).wait_send()
        for k in range(1, NX):
            vx(k).wait_send()
            hx(k).wait_send()
            for j in range(MP):
                wx(j, k).wait_send()
                gx(j, k).wait_send()
        for j in range(MP):
            wc(j).wait_send()
            gc(j).wait_send()
        vc().wait_send()
        hc().wait_send()
    for wait in sends:
        wait()


def expert_grad_kernel(slots, dpre, hidden, dresults, in_grad, out_grad):
    in_grad[0] = tn(slots[0], dpre[0])
    out_grad[0] = tn(hidden[0], dresults[0])


def per_device(mesh, tokens, norm_params, w_qkv, w_proj, phi, w_in, w_out, cotangent):
    z = Sizes(mesh, tokens, w_qkv, phi, w_in)
    vmem, anyspace = pl.BlockSpec(memory_space=pltpu.VMEM), pl.BlockSpec(memory_space=pl.ANY)
    inputs = dict(
        tokens=tokens, norm_params=norm_params, w_qkv=w_qkv, w_proj=w_proj, phi=phi, cotangent=cotangent
    )
    specs = [vmem] * len(inputs)
    inputs.update(w_in=w_in, w_out=w_out)
    specs += [anyspace] * 2
    images = z.MP * z.DP
    outs = dict(
        output=((z.ROWS, z.CW), F32), input_grad=((z.ROWS, z.CW), F32),
        phi_grad=((z.E, z.D), F32), norm_grad=((4, z.D), F32),
        slots=((z.EPD, images, z.D), BF), dresults=((z.EPD, images, z.D), BF),
        hidden=((z.EPD, images, z.F), BF), dpre=((z.EPD, images, z.F), BF),
    )
    if z.own_weights:
        outs.update(qkv_grad=((3, z.RB, z.CW), F32), proj_grad=((z.CW, z.RB), F32))
    else:
        outs.update(gq=((z.MP, z.D, z.QW), BF), gp=((z.MP, z.D, z.CW), BF))
        wall = lax.all_gather(w_qkv.astype(BF), "dp", axis=1, tiled=True)
        wall = jnp.concatenate([wall[c] for c in range(3)], axis=1)
        wpall = lax.all_gather(w_proj.T.astype(BF), "dp", axis=0, tiled=True)
        inputs.update(wall=lax.all_gather(wall, "mp"), wpall=lax.all_gather(wpall, "mp"))
        specs += [vmem] * 2
    names, scratch = scratch_of(z)
    result = pl.pallas_call(
        functools.partial(block_kernel, z, list(inputs), list(outs), names),
        out_shape=[jax.ShapeDtypeStruct(*one) for one in outs.values()],
        in_specs=specs,
        out_specs=[vmem] * len(outs),
        scratch_shapes=scratch,
        compiler_params=pltpu.CompilerParams(
            collective_id=0, has_side_effects=True, vmem_limit_bytes=62 * 2**20
        ),
        name="block",
    )(*inputs.values())
    got = dict(zip(outs, result))

    pieces = 3

    def rows_in(e, i):
        return (e, 0, i)

    in_grad, out_grad = pl.pallas_call(
        expert_grad_kernel,
        grid=(z.EPD, pieces),
        in_specs=[
            pl.BlockSpec((1, images, z.D // pieces), rows_in),
            pl.BlockSpec((1, images, z.F), lambda e, i: (e, 0, 0)),
            pl.BlockSpec((1, images, z.F // pieces), rows_in),
            pl.BlockSpec((1, images, z.D), lambda e, i: (e, 0, 0)),
        ],
        out_specs=[
            pl.BlockSpec((1, z.D // pieces, z.F), lambda e, i: (e, i, 0)),
            pl.BlockSpec((1, z.F // pieces, z.D), lambda e, i: (e, i, 0)),
        ],
        out_shape=[
            jax.ShapeDtypeStruct((z.EPD, z.D, z.F), F32),
            jax.ShapeDtypeStruct((z.EPD, z.F, z.D), F32),
        ],
        name="expert_grads",
    )(got["slots"], got["dpre"], got["hidden"], got["dresults"])

    phi_grad, norm_grad = got["phi_grad"].T, got["norm_grad"]
    if z.own_weights:
        qkv_grad, proj_grad = got["qkv_grad"], got["proj_grad"]
    else:
        phi_grad, norm_grad = lax.psum((phi_grad, norm_grad), ("dp", "mp"))
        gq = lax.psum_scatter(got["gq"].astype(F32), "mp", scatter_dimension=0, tiled=False)
        gp = lax.psum_scatter(got["gp"].astype(F32), "mp", scatter_dimension=0, tiled=False)
        gq = jnp.stack([gq[:, c * z.CW : (c + 1) * z.CW] for c in range(3)])
        qkv_grad = lax.psum_scatter(gq, "dp", scatter_dimension=1, tiled=True)
        proj_grad = lax.psum_scatter(gp, "dp", scatter_dimension=0, tiled=True).T
    return (
        got["output"], got["input_grad"], qkv_grad, proj_grad, in_grad, out_grad, phi_grad, norm_grad
    )


def solution(mesh):
    return jax.shard_map(
        functools.partial(per_device, mesh),
        mesh=mesh,
        in_specs=(
            P("dp", "mp"), P(), P(None, "dp", "mp"), P("mp", "dp"), P(),
            P("dp", None, "mp"), P("dp", "mp", None), P("dp", "mp"),
        ),
        out_specs=(
            P("dp", "mp"), P("dp", "mp"), P(None, "dp", "mp"), P("mp", "dp"),
            P("dp", None, "mp"), P("dp", "mp", None), P(), P(),
        ),
        check_vma=False,
    )
```

time: 487 us -> 161 us (0.33)
  waiting for transfers between devices: 246 us -> 0 us
  Pallas kernels: 0 us -> 144 us
  blocking collectives: 73.6 us -> 0 us
  matrix products: 56.7 us -> 0 us
  local copies, waits for them, and re-layouts: 62.1 us -> 16 us
  other arithmetic: 16.1 us -> 0 us
  starting transfers between devices: 15.6 us -> 0 us
  between operations: 14.8 us -> 0.65 us
    psum x2 -> x0, waiting for transfers between devices: 193 us -> none  [the longest x1 98.1 us: per_device(): grad_first = lax.psum(first_grad_part, 'mp')]
    pallas_call x0 -> x2, Pallas kernels: none -> 144 us  [the longest x1 138 us: per_device(): pl.pallas_call(functools.partial(block_kernel, z, list(inputs), list(outs...]
    dot_general x24 -> x0, matrix products: 50.6 us -> none  [the longest x1 4.43 us: per_device(): jnp.einsum('te,de->td', logits_low, phi_low, preferred_element_type=jnp.f...]
    psum x2 -> x0, blocking collectives: 50.4 us -> none  [the longest x1 25.3 us: per_device(): phi_grad, norm_grad = lax.psum((phi_part, norm_part), 'dp')]
    all_gather x2 -> x0, waiting for transfers between devices: 30 us -> none  [the longest x1 18.8 us: per_device(): lax.all_gather(cotangent, 'mp', axis=1, tiled=True)]
    all_gather x2 -> x0, blocking collectives: 23.2 us -> none  [the longest x1 14.6 us: per_device(): lax.all_gather(qkv_local, 'dp', axis=1, tiled=True)]
    all_to_all x4 -> x0, starting transfers between devices: 15.2 us -> none  [the longest x1 3.98 us: per_device(): lax.all_to_all(slot_grad, 'dp', split_axis=0, concat_axis=1, tiled=True)]
    unnamed x8 -> x0, waiting for transfers between devices: 15 us -> none
  transfers between devices with their start and end apart: 10 -> 0, of which waited for: 9 -> 0; matrix products, arithmetic and copies ran while one was open for 14% -> 0% of each run, Pallas kernels for 0% -> 0%
where the time goes in v1:
time: 161 us; the launch traced here: 160 us
  Pallas kernels  144 us (89%)
  local copies, waits for them, and re-layouts  16 us (10%)
    pallas_call x1, Pallas kernels, per_device(): pl.pallas_call(functools.partial(block_kernel, z, list(inputs), list(outs...  138 us
    unnamed x9, local copies, waits for them, and re-layouts  16 us
    pallas_call x1, Pallas kernels, per_device(): pl.pallas_call(expert_grad_kernel, grid=(z.EPD, pieces), in_specs=[pl.Blo...  6.03 us

profile of v1, /device:TPU:0, one launch (start us, length us, event | category | flops | bytes accessed | tf_op | source)
XLA Modules:
  0.0 160.4 jit_solution(10240548993536011350)
XLA Ops:
  0.6 1.7 %copy.17.refs_4_ = f32[768,16]{1,0:T(8,128)} copy(f32[768,16]{0,1:T(8,128)} %param.12) | data formatting | bytes 98304 | tf_op args[4]
  2.3 1.9 %copy.16.refs_0_ = bf16[784,192]{1,0:T(8,128)(2,1)} copy(bf16[784,192]{0,1:T(8,128)(2,1)} %param.8) | data formatting | bytes 602112 | tf_op args[0]
  4.2 1.9 %copy.18.refs_5_ = bf16[784,192]{1,0:T(8,128)(2,1)} copy(bf16[784,192]{0,1:T(8,128)(2,1)} %param.15) | data formatting | bytes 602112 | tf_op args[7]
  6.2 137.7 %block.1 = (f32[784,192]{1,0:T(8,128)}, f32[784,192]{1,0:T(8,128)}, f32[16,768]{1,0:T(8,128)}, f32[4,768]{1,0:T(4,128)}, bf16[2,32,768]{2,1,0:T(8,128)(2,1)}, /*...) custom-call(bf16[784,192]{1,0:T(8,128)(2,1)} %copy.16.refs_0_, ...), custom_call_target="tpu_custom_call" | custom-call | tf_op jit(solution)/shard_map/block/pallas_call | solution.py:720
  143.9 2.3 %copy.19 = f32[784,192]{0,1:T(8,128)} copy(f32[784,192]{1,0:T(8,128)} %get-tuple-element.32) | data formatting | bytes 1204224
  146.2 2.3 %copy.20 = f32[784,192]{0,1:T(8,128)} copy(f32[784,192]{1,0:T(8,128)} %get-tuple-element.33) | data formatting | bytes 1204224
  148.4 6.0 %expert_grads.1 = (f32[2,768,768]{2,1,0:T(8,128)}, f32[2,768,768]{2,1,0:T(8,128)}) custom-call(bf16[2,32,768]{2,1,0:T(8,128)(2,1)} %get-tuple-element.24.slots, bf16[2,32,768]{2,1,0:T(8,128)(2,1)} %get-tuple-element.25.dpre, bf16[2,32,768]{2,1,0:T(8,128)(2,1)} %get-tuple-element.26.hidden, bf16[2,32,768]{2,1,0:T(8,128)(2,1)} %get-tuple-element.27.dresults), custom_call_target="tpu_custom_call" | custom-call | tf_op jit(solution)/shard_map/expert_grads/pallas_call | solution.py:738
  154.5 1.7 %copy.25 = f32[3,96,192]{2,1,0:T(8,128)} copy(f32[3,96,192]{2,1,0:T(8,128)} %get-tuple-element.50) | data formatting | bytes 442368
  156.2 1.5 copy.26
  157.7 1.4 copy.27
  159.1 1.3 copy.28

commit v2 on v1

v2 whole, which is shorter than its diff:
```python
import functools
import math

import jax
import jax.numpy as jnp
from jax import lax
from jax.experimental import pallas as pl
from jax.experimental.pallas import tpu as pltpu
from jax.sharding import PartitionSpec as P

HEAD_DIM = 64
SEQ = 196
EPSILON = 1e-06
MESH = pl.DeviceIdType.MESH
BF = jnp.bfloat16
F32 = jnp.float32
NEG = -1e30


def nn(a, b):
    return lax.dot_general(a, b, (((1,), (0,)), ((), ())), preferred_element_type=F32)


def nt(a, b):
    return lax.dot_general(a, b, (((1,), (1,)), ((), ())), preferred_element_type=F32)


def tn(a, b):
    return lax.dot_general(a, b, (((0,), (0,)), ((), ())), preferred_element_type=F32)


def each(low, high, body):
    if high - low <= 8:
        for i in range(low, high):
            body(i)
    else:

        def step(i, carry):
            body(i)
            return carry

        lax.fori_loop(low, high, step, 0)


def select_rows(rows, cols, source):
    row = lax.broadcasted_iota(jnp.int32, (rows, cols), 0)
    col = lax.broadcasted_iota(jnp.int32, (rows, cols), 1)
    return jnp.where(col == source(row), 1.0, 0.0).astype(BF)


def normalize(values):
    mean = jnp.mean(values, axis=-1, keepdims=True)
    centered = values - mean
    var = jnp.mean(centered * centered, axis=-1, keepdims=True)
    inv = lax.rsqrt(var + EPSILON)
    return centered * inv, inv


def norm_backward(grad, gain, normed, inv):
    scaled = grad * gain
    first = jnp.mean(scaled, axis=-1, keepdims=True)
    second = jnp.mean(scaled * normed, axis=-1, keepdims=True)
    return inv * (scaled - first - normed * second)


class Sizes:
    def __init__(self, mesh, tokens, w_qkv, phi, w_in):
        self.DP, self.MP = mesh.shape["dp"], mesh.shape["mp"]
        self.D, self.E = phi.shape
        self.CW = tokens.shape[1]
        self.RB = w_qkv.shape[1]
        self.QW = 3 * self.CW
        self.HL = self.CW // HEAD_DIM
        self.EPD = w_in.shape[0]
        self.F = w_in.shape[2]
        self.IN = 2
        self.NX = self.DP // self.IN
        self.SP = (SEQ + 15) // 16 * 16
        self.ROWS = tokens.shape[0]
        self.KE = 2 * self.EPD
        self.own_weights = self.NX == 4 and self.RB % 32 == 0 and self.E + 2 <= self.KE * self.DP


def scratch_of(z):
    dma = pltpu.SemaphoreType.DMA
    v = pltpu.VMEM
    DP, MP, D, CW, RB, QW, SP, NX, IN, KE = z.DP, z.MP, z.D, z.CW, z.RB, z.QW, z.SP, z.NX, z.IN, z.KE
    half = RB // 2
    items = dict(
        tsend=v((MP, SP, CW), BF), tin=v((MP, SP, CW), BF),
        csend=v((MP, SP, CW), BF), cin=v((MP, SP, CW), BF),
        osend=v((MP, SP, CW), BF), oin=v((MP, SP, CW), BF),
        isend=v((MP, SP, CW), BF),
        wf_in=v((z.EPD, D, z.F), F32), wf_out=v((z.EPD, z.F, D), F32),
        wb_in=v((z.EPD, D, z.F), BF), wb_out=v((z.EPD, z.F, D), BF),
        h1=v((SP, D), BF), qkv=v((MP, SP, QW), BF), probs=v((MP, z.HL, SP, SP), F32),
        att=v((MP, SP, CW), BF), datt=v((MP, SP, CW), BF),
        resid=v((SP, D), F32), dresid=v((SP, D), F32), dh1=v((SP, D), F32),
        slot_out=v((DP, KE, D), F32), slot_in=v((DP, KE, D), F32),
        slot_all=v((MP, KE * DP, D), BF),
        part=v((MP, KE * DP, D), F32), psend=v((MP, KE * DP, D), BF), pin=v((MP, KE * DP, D), BF),
        back_out=v((DP, KE, D), F32), back_in=v((DP, KE, D), F32),
    )
    sems = dict(
        tok=(2, MP), cot=(2, MP), outs=(2, MP), ings=(2, MP), hbm=(2,),
        dp1=(2, DP), mp1=(2, 2, MP), mp2=(2, 2, MP), dp2=(2, DP),
    )
    if z.own_weights:
        items.update(
            wall=v((MP, NX, IN, RB, QW), BF), wpall=v((MP, NX, IN, RB, CW), BF),
            gq=v((MP, NX, IN, RB, QW), BF), gp=v((NX, IN, RB, D), BF),
            cq=v((MP, NX, RB, QW), BF), cp=v((NX, RB, D), BF),
            xq=v((MP, NX, RB, QW), BF), xp=v((NX, RB, D), BF),
            aq=v((MP, 4, half, QW), BF), ap=v((4, half, D), BF),
            bq=v((MP, 2, half, QW), BF), bp=v((2, half, D), BF),
            dq=v((MP, 2, half, QW), BF), dp_=v((2, half, D), BF),
            zq=v((MP, RB, QW), BF), rq=v((MP, RB, QW), BF),
            fp=v((MP, RB, CW), F32), zp=v((MP, RB, CW), BF), rp=v((MP, RB, CW), BF),
            sa=v((DP, KE, D), F32), sb=v((DP, KE, D), F32), sc=v((MP, KE, D), F32), sd=v((DP, KE, D), F32),
            ta=v((2, D), F32), tb=v((DP, 2, D), F32), tc=v((MP, 2, D), F32),
        )
        sems.update(
            wz=(2, MP), wx=(2, MP, 4), wc=(2, MP), vz=(2, MP), vx=(2, 4), vc=(2,),
            gc=(2, MP), gx=(2, MP, 6), gz=(2, MP), hc=(2,), hx=(2, 6), hz=(2, MP),
            s1=(2, DP), s2=(2, MP), s3=(2, DP), t1=(2, DP), t2=(2, MP),
        )
    names, shapes = [], []
    for name, shape in items.items():
        names.append(name)
        shapes.append(shape)
    for name, shape in sems.items():
        names.append("m_" + name)
        shapes.append(dma(shape))
    return names, shapes


class Refs:
    pass


def block_kernel(z, in_names, out_names, names, *refs):
    r = Refs()
    for name, ref in zip(in_names + out_names + names, refs):
        setattr(r, name, ref)
    DP, MP, D, CW, RB, QW, SP = z.DP, z.MP, z.D, z.CW, z.RB, z.QW, z.SP
    NX, IN, E, EPD, KE = z.NX, z.IN, z.E, z.EPD, z.KE
    half = RB // 2
    dp, mp = lax.axis_index("dp"), lax.axis_index("mp")
    xy, co = dp // IN, lax.rem(dp, IN)
    xn = xy + 1 - 2 * lax.rem(xy, 2)
    yn = lax.rem(xy + 2, NX)
    dg = lax.rem(xn + 2, NX)
    to_x, to_y, to_core = (xn * IN + co, mp), (yn * IN + co, mp), (xy * IN + 1 - co, mp)
    sends = []

    def remote(src, dst, sem, s_at, r_at, device):
        return pltpu.make_async_remote_copy(
            src_ref=src, dst_ref=dst, send_sem=sem.at[(0,) + s_at], recv_sem=sem.at[(1,) + r_at],
            device_id=device, device_id_type=MESH,
        )

    def send(*copy):
        remote(*copy).start()
        sends.append(lambda: remote(*copy).wait_send())

    def arrive(ref, sem, at):
        remote(ref, ref, sem, at, at, to_mp(1)).wait_recv()

    def mp_at(k):
        return lax.rem(mp + k, MP)

    def dp_at(k):
        return lax.rem(dp + k, DP)

    def to_mp(k):
        return (dp, mp_at(k))

    def to_dp(k):
        return (dp_at(k), mp)

    barrier = pltpu.get_barrier_semaphore()
    for k in range(1, MP):
        pl.semaphore_signal(barrier, inc=1, device_id=to_mp(k), device_id_type=MESH)
    each(1, DP, lambda k: pl.semaphore_signal(barrier, inc=1, device_id=to_dp(k), device_id_type=MESH))

    load_in = pltpu.make_async_copy(r.w_in, r.wf_in, r.m_hbm.at[0])
    load_out = pltpu.make_async_copy(r.w_out, r.wf_out, r.m_hbm.at[1])
    load_in.start()
    load_out.start()

    if z.own_weights:
        r.wall[mp, xy, co] = jnp.concatenate([r.w_qkv[c].astype(BF) for c in range(3)], axis=1)
        r.wpall[mp, xy, co] = r.w_proj[...].T.astype(BF)
    pl.semaphore_wait(barrier, MP - 1 + DP - 1)

    def to_images(source, target):
        target[...] = jnp.zeros((MP, SP, CW), BF)
        rows = source[...].T
        for i in range(MP):
            target[i, 0:SEQ, :] = rows[SEQ * i : SEQ * (i + 1)]

    def swap(src, dst, sem):
        for k in range(1, MP):
            send(src.at[mp_at(k)], dst.at[mp], sem, (k,), (MP - k,), to_mp(k))
        dst[mp] = src[mp]

    def swap_wait(dst, sem):
        for k in range(1, MP):
            arrive(dst.at[mp_at(k)], sem, (k,))

    def to_column(block, sem):
        for k in range(1, MP):
            send(block, block, sem, (k,), (MP - k,), to_mp(k))

    class Plane:
        def __init__(self, block, sem, at):
            self.block, self.sem, self.at = block, sem, at

        def copy(self, ref, way, device):
            send(ref, ref, self.sem, self.at + (way,), self.at + (way,), device)

        def start(self):
            self.copy(self.block(xy, 0, RB), 0, to_x)
            self.copy(self.block(xy, 0, RB), 1, to_y)

        def forward(self):
            arrive(self.block(xn, 0, RB), self.sem, self.at + (0,))
            self.copy(self.block(xn, 0, half), 2, to_y)
            arrive(self.block(yn, 0, RB), self.sem, self.at + (1,))
            self.copy(self.block(yn, half, half), 3, to_x)

        def wait(self):
            arrive(self.block(dg, 0, half), self.sem, self.at + (2,))
            arrive(self.block(dg, half, half), self.sem, self.at + (3,))

    def qkv_plane(j):
        return Plane(lambda pos, low, rows: r.wall.at[mp_at(j), pos, co, pl.ds(low, rows)], r.m_wx, (j,))

    def other_core(ref, core, sem, at):
        send(ref(core), ref(core), sem, at, at, to_core)

    def qkv_cores(j):
        return lambda core: r.wall.at[mp_at(j), :, core]

    def load_expert(copy, wide, low):
        copy.wait()
        low[...] = wide[...].astype(BF)

    if z.own_weights:
        planes = [qkv_plane(j) for j in range(MP)]
        proj_plane = Plane(lambda pos, low, rows: r.wpall.at[:, pos, co, pl.ds(low, rows)], r.m_vx, ())

        def column_arrived(j):
            arrive(r.wall.at[mp_at(j), xy, co], r.m_wz, (j,))
            planes[j].start()

        def plane_arrived(j):
            planes[j].wait()
            other_core(qkv_cores(j), co, r.m_wc, (j,))

        to_column(r.wall.at[mp, xy, co], r.m_wz)
        planes[0].start()
        to_column(r.wpall.at[mp, xy, co], r.m_vz)
        to_images(r.tokens, r.tsend)
        load_expert(load_in, r.wf_in, r.wb_in)
        column_arrived(1)
        planes[0].forward()
        column_arrived(2)
        planes[1].forward()
        plane_arrived(0)
        column_arrived(3)
        swap(r.tsend, r.tin, r.m_tok)
        planes[2].forward()
        plane_arrived(1)
        for k in range(1, MP):
            arrive(r.wpall.at[mp_at(k), xy, co], r.m_vz, (k,))
        proj_plane.start()
        to_images(r.cotangent, r.csend)
        planes[3].forward()
        plane_arrived(2)
        load_expert(load_out, r.wf_out, r.wb_out)
        swap(r.csend, r.cin, r.m_cot)
        proj_plane.forward()
        plane_arrived(3)
    else:
        to_images(r.tokens, r.tsend)
        swap(r.tsend, r.tin, r.m_tok)
        to_images(r.cotangent, r.csend)
        swap(r.csend, r.cin, r.m_cot)
        load_expert(load_in, r.wf_in, r.wb_in)
        load_expert(load_out, r.wf_out, r.wb_out)

    swap_wait(r.tin, r.m_tok)
    gain1, shift1 = r.norm_params[0:1, :], r.norm_params[1:2, :]
    gain2, shift2 = r.norm_params[2:3, :], r.norm_params[3:4, :]

    def own_image(ref):
        return jnp.concatenate([ref[i] for i in range(MP)], axis=1)

    normed1, _ = normalize(own_image(r.tin).astype(F32))
    r.h1[...] = (normed1 * gain1 + shift1).astype(BF)

    scale = 1.0 / math.sqrt(HEAD_DIM)
    key_ok = lax.broadcasted_iota(jnp.int32, (1, SP), 1) < SEQ

    def weight(m):
        return r.wall[m].reshape(D, QW) if z.own_weights else r.wall[m]

    def proj_weight(m):
        return r.wpall[m].reshape(D, CW) if z.own_weights else r.wpall[m]

    def head_cols(qkv, h):
        return (qkv[:, c * CW + h * HEAD_DIM : c * CW + (h + 1) * HEAD_DIM] for c in range(3))

    def heads_forward(j, carry):
        m = mp_at(j)
        if z.own_weights:
            arrive(r.wall.at[m, :, 1 - co], r.m_wc, (j,))

            @pl.when(j == MP - 1)
            def _():
                proj_plane.wait()
                remote(r.wpall.at[:, :, co], r.wpall.at[:, :, co], r.m_vc, (), (), to_core).start()

        qkv = nn(r.h1[...], weight(m)).astype(BF)
        r.qkv[m] = qkv
        attended = []
        for h in range(z.HL):
            query, key, value = head_cols(qkv, h)
            scores = jnp.where(key_ok, nt(query, key) * scale, NEG)
            top = jnp.max(scores, axis=-1, keepdims=True)
            grown = jnp.exp(scores - top)
            probs = grown / jnp.sum(grown, axis=-1, keepdims=True)
            r.probs[m, h] = probs
            attended.append(nn(probs.astype(BF), value))
        r.att[m] = jnp.concatenate(attended, axis=1).astype(BF)
        return carry

    lax.fori_loop(0, MP, heads_forward, 0)
    if z.own_weights:
        sends.append(lambda: remote(r.wpall.at[:, :, co], r.wpall.at[:, :, co], r.m_vc, (), (), to_core).wait_send())
        arrive(r.wpall.at[:, :, 1 - co], r.m_vc, ())

    resid = own_image(r.tin).astype(F32)
    for m in range(MP):
        resid = resid + nt(r.att[m], proj_weight(m))
    r.resid[...] = resid
    normed2, inv2 = normalize(resid)
    h2 = (normed2 * gain2 + shift2).astype(BF)
    phi_low = r.phi[...].astype(BF)
    logits = nt(h2, phi_low)
    token_ok = lax.broadcasted_iota(jnp.int32, (SP, 1), 0) < SEQ
    masked = jnp.where(token_ok, logits, NEG)
    grown = jnp.exp(masked - jnp.max(masked, axis=0, keepdims=True))
    dispatch = grown / jnp.sum(grown, axis=0, keepdims=True)
    grown = jnp.exp(logits - jnp.max(logits, axis=1, keepdims=True))
    combine = grown / jnp.sum(grown, axis=1, keepdims=True)
    dispatch_low, combine_low = dispatch.astype(BF), combine.astype(BF)
    swap_wait(r.cin, r.m_cot)
    grad = own_image(r.cin)
    slots = tn(dispatch_low, h2).astype(BF)
    dresults = tn(combine_low, grad).astype(BF)

    def spread(target, rows):
        for d in range(DP):
            target[d] = rows[d * KE : (d + 1) * KE]

    def collect(source):
        return jnp.concatenate([source[d] for d in range(DP)], axis=0)

    def dp_swap(src, dst, sem):
        def copy(k):
            return remote(src.at[dp_at(k)], dst.at[dp], sem, (k,), (DP - k,), to_dp(k))

        each(1, DP, lambda k: copy(k).start())
        sends.append(lambda: each(1, DP, lambda k: copy(k).wait_send()))
        dst[dp] = src[dp]

    def dp_wait(dst, sem):
        each(1, DP, lambda k: arrive(dst.at[dp_at(k)], sem, (k,)))

    def out_row(row):
        d, q = row // KE, row % KE
        return (q // EPD) * E + d * EPD + q % EPD

    spread(r.slot_out, nn(select_rows(DP * KE, 2 * E, out_row), jnp.concatenate([slots, dresults], axis=0)))
    dp_swap(r.slot_out, r.slot_in, r.m_dp1)
    dp_wait(r.slot_in, r.m_dp1)
    gather_rows = select_rows(KE * DP, DP * KE, lambda row: (row % DP) * KE + row // DP)
    r.slot_all[mp] = nn(gather_rows, collect(r.slot_in).astype(BF)).astype(BF)
    rows = EPD * DP

    def kind_rows(ref, kind):
        return ref.at[pl.ds(kind * rows, rows)]

    for kind in range(2):
        for k in range(1, MP):
            block = kind_rows(r.slot_all.at[mp], kind)
            send(block, block, r.m_mp1, (kind, k), (kind, MP - k), to_mp(k))

    def expert_rows(kind):
        for k in range(1, MP):
            arrive(kind_rows(r.slot_all.at[mp_at(k)], kind), r.m_mp1, (kind, k))
        parts = [r.slot_all[m, kind * rows : (kind + 1) * rows, :].astype(F32) for m in range(MP)]
        return [
            jnp.concatenate([one[e * DP : (e + 1) * DP] for one in parts], axis=0).astype(BF) for e in range(EPD)
        ]

    def send_parts(kind, per_expert):
        for e in range(EPD):
            at = kind * rows + e * DP
            for m in range(MP):
                r.part[m, at : at + DP, :] = per_expert[e][m * DP : (m + 1) * DP]
        here = slice(kind * rows, (kind + 1) * rows)
        r.psend[:, here, :] = r.part[:, here, :].astype(BF)
        for k in range(1, MP):
            send(
                kind_rows(r.psend.at[mp_at(k)], kind), kind_rows(r.pin.at[MP - k], kind),
                r.m_mp2, (kind, k), (kind, MP - k), to_mp(k),
            )

    slopes, results_part = [], []
    for e, slots_e in enumerate(expert_rows(0)):
        pre = nn(slots_e, r.wb_in[e])
        cdf = 0.5 * (1.0 + lax.erf(pre * (1.0 / math.sqrt(2.0))))
        hidden = (pre * cdf).astype(BF)
        results_part.append(nn(hidden, r.wb_out[e]))
        slopes.append(cdf + pre * jnp.exp(-0.5 * pre * pre) * (1.0 / math.sqrt(2.0 * math.pi)))
        r.slots[e], r.hidden[e] = slots_e, hidden
    send_parts(0, results_part)
    dslots_part = []
    for e, dresults_e in enumerate(expert_rows(1)):
        dpre = (nt(dresults_e, r.wb_out[e]) * slopes[e]).astype(BF)
        dslots_part.append(nt(dpre, r.wb_in[e]))
        r.dresults[e], r.dpre[e] = dresults_e, dpre
    send_parts(1, dslots_part)
    total = r.part[mp]
    for k in range(1, MP):
        for kind in range(2):
            arrive(kind_rows(r.pin.at[k], kind), r.m_mp2, (kind, k))
        total = total + r.pin[k].astype(F32)
    back_rows = select_rows(DP * KE, KE * DP, lambda row: (row % KE) * DP + row // KE)
    spread(r.back_out, nn(back_rows, total.astype(BF)))
    dp_swap(r.back_out, r.back_in, r.m_dp2)
    dp_wait(r.back_in, r.m_dp2)

    def result_row(row):
        kind, e = row // E, row % E
        return (e // EPD) * KE + kind * EPD + e % EPD

    both = nn(select_rows(2 * E, DP * KE, result_row), collect(r.back_in).astype(BF)).astype(BF)
    results, dslots = both[:E], both[E:]

    output = r.resid[...] + nn(combine_low, results)
    for m in range(MP):
        r.osend[m] = output[:, m * CW : (m + 1) * CW].astype(BF)
    swap(r.osend, r.oin, r.m_outs)
    dcombine, ddispatch = nt(grad, results), nt(h2, dslots)
    dlogits = dispatch * (ddispatch - jnp.sum(dispatch * ddispatch, axis=0, keepdims=True))
    dlogits = dlogits + combine * (dcombine - jnp.sum(combine * dcombine, axis=1, keepdims=True))
    dlogits = dlogits.astype(BF)
    dh2 = nn(dispatch_low, dslots) + nn(dlogits, phi_low)
    dresid = grad.astype(F32) + norm_backward(dh2, gain2, normed2, inv2)
    r.dresid[...] = dresid
    dbranch = dresid.astype(BF)
    proj_part = tn(dbranch, own_image(r.att)).astype(BF)

    class Unit:
        def __init__(self, part, got, mine, first, out, second, core_sem, sem, at):
            self.part, self.got, self.mine, self.first = part, got, mine, first
            self.out, self.second, self.core_sem, self.sem, self.at = out, second, core_sem, sem, at

        def start(self):
            send(self.part.at[:, 1 - co], self.got, self.core_sem, self.at, self.at, to_core)

        def copy(self, src, dst, way, device):
            send(src, dst, self.sem, self.at + (way,), self.at + (way,), device)

        def plane(self):
            arrive(self.got, self.core_sem, self.at)
            for x in range(NX):
                self.mine[x] = (self.part[x, co].astype(F32) + self.got[x].astype(F32)).astype(BF)
            low, high = pl.ds(0, half), pl.ds(half, half)
            self.copy(self.mine.at[dg, low], self.first.at[1], 1, to_x)
            self.copy(self.mine.at[dg, high], self.first.at[3], 3, to_y)
            self.copy(self.mine.at[xn, low], self.first.at[0], 0, to_x)
            self.copy(self.mine.at[yn, high], self.first.at[2], 2, to_y)

        def added(self, x, low, index):
            arrive(self.first.at[index], self.sem, self.at + (index,))
            return self.mine[x, low : low + half, :].astype(F32) + self.first[index].astype(F32)

        def forward(self):
            self.out[0] = self.added(yn, 0, 1).astype(BF)
            self.copy(self.out.at[0], self.second.at[0], 4, to_y)
            self.out[1] = self.added(xn, half, 3).astype(BF)
            self.copy(self.out.at[1], self.second.at[1], 5, to_x)

        def total(self):
            pieces = []
            for i in range(2):
                piece = self.added(xy, i * half, 2 * i)
                arrive(self.second.at[i], self.sem, self.at + (4 + i,))
                pieces.append(piece + self.second[i].astype(F32))
            return jnp.concatenate(pieces, axis=0)

    def qkv_unit(j):
        return Unit(
            r.gq.at[mp_at(j)], r.cq.at[j], r.xq.at[j], r.aq.at[j], r.bq.at[j], r.dq.at[j], r.m_gc, r.m_gx, (j,)
        )

    def qkv_column(j):
        r.zq[j] = units[j].total().astype(BF)
        send(r.zq.at[j], r.rq.at[MP - j], r.m_gz, (j,), (MP - j,), to_mp(j))

    def proj_column():
        total = proj_unit.total()
        for m in range(MP):
            piece = total[:, m * CW : (m + 1) * CW]
            r.fp[m] = piece
            r.zp[m] = piece.astype(BF)
        for k in range(1, MP):
            send(r.zp.at[mp_at(k)], r.rp.at[MP - k], r.m_hz, (k,), (MP - k,), to_mp(k))

    def sum_of(ref, count):
        total = ref[0]
        for i in range(1, count):
            total = total + ref[i]
        return total

    def small_column():
        dp_wait(r.sb, r.m_s1)
        r.sc[mp] = sum_of(r.sb, DP)
        to_column(r.sc.at[mp], r.m_s2)

    def small_back():
        for k in range(1, MP):
            arrive(r.sc.at[mp_at(k)], r.m_s2, (k,))
        r.sd[dp] = sum_of(r.sc, MP)
        for k in range(1, DP):
            send(r.sd.at[dp], r.sd.at[dp], r.m_s3, (k,), (DP - k,), to_dp(k))

    def gains(grad_out, normed):
        return jnp.concatenate(
            [jnp.sum(grad_out * normed, axis=0, keepdims=True), jnp.sum(grad_out, axis=0, keepdims=True)], axis=0
        )

    if z.own_weights:
        units = [qkv_unit(j) for j in range(MP)]
        proj_unit = Unit(r.gp, r.cp, r.xp, r.ap, r.bp, r.dp_, r.m_hc, r.m_hx, ())
        r.gp[...] = proj_part.reshape(NX, IN, RB, D)
        proj_unit.start()
    else:
        r.gp[...] = proj_part
    for m in range(MP):
        r.datt[m] = nn(dbranch, proj_weight(m)).astype(BF)
    rows2 = gains(dh2, normed2)
    if z.own_weights:
        phi_part = tn(dlogits, h2)
        r.sa[...] = jnp.zeros((DP, KE, D), F32)
        for i in range(E // KE):
            r.sa[i] = phi_part[i * KE : (i + 1) * KE]
        r.sa[E // KE, 0:2, :] = rows2
        dp_swap(r.sa, r.sb, r.m_s1)
    else:
        r.phi_grad[...] = tn(dlogits, h2)

    def heads_backward(j):
        m = mp_at(j)
        qkv, datt = r.qkv[m], r.datt[m]
        pieces = [[], [], []]
        for h in range(z.HL):
            query, key, value = head_cols(qkv, h)
            grad_h = datt[:, h * HEAD_DIM : (h + 1) * HEAD_DIM]
            probs = r.probs[m, h]
            dprobs = nt(grad_h, value)
            dscores = probs * (dprobs - jnp.sum(probs * dprobs, axis=-1, keepdims=True))
            dscores = dscores.astype(BF)
            pieces[0].append(nn(dscores, key) * scale)
            pieces[1].append(tn(dscores, query) * scale)
            pieces[2].append(tn(probs.astype(BF), grad_h))
        dqkv = jnp.concatenate(pieces[0] + pieces[1] + pieces[2], axis=1).astype(BF)
        piece = tn(r.h1[...], dqkv).astype(BF)
        if z.own_weights:
            r.gq[m] = piece.reshape(NX, IN, RB, QW)
        else:
            r.gq[m] = piece
        return dqkv

    order = list(range(1, MP)) + [0]
    between = {0: [], 1: [], 2: [], 3: []}
    if z.own_weights:
        between = {
            0: [proj_unit.plane],
            1: [units[1].plane, proj_unit.forward],
            2: [units[2].plane, units[1].forward, small_column],
            3: [units[3].plane, units[2].forward, proj_column],
        }
    dh1 = None
    for i, j in enumerate(order):
        dqkv = heads_backward(j)
        if z.own_weights:
            units[j].start()
        part = nt(dqkv, weight(mp_at(j)))
        if i == 0:
            r.dh1[...] = part
        else:
            r.dh1[...] += part
        for step in between.get(i, []):
            step()

    if z.own_weights:
        units[0].plane()
    normed1, inv1 = normalize(own_image(r.tin).astype(F32))
    dh1 = r.dh1[...]
    rows1 = gains(dh1, normed1)
    if z.own_weights:
        r.ta[...] = rows1
        for k in range(1, DP):
            send(r.ta, r.tb.at[dp], r.m_t1, (k,), (DP - k,), to_dp(k))
        r.tb[dp] = rows1
    input_grad = r.dresid[...] + norm_backward(dh1, gain1, normed1, inv1)
    for m in range(MP):
        r.isend[m] = input_grad[:, m * CW : (m + 1) * CW].astype(BF)
    swap(r.isend, r.iin, r.m_ings)

    if z.own_weights:
        qkv_column(1)
        units[3].forward()
        small_back()
        qkv_column(2)
        units[0].forward()
        dp_wait(r.tb, r.m_t1)
        r.tc[mp] = sum_of(r.tb, DP)
        to_column(r.tc.at[mp], r.m_t2)
    swap_wait(r.oin, r.m_outs)
    r.output[...] = from_images(r.oin)
    if z.own_weights:
        qkv_column(3)
        total = r.fp[mp]
        for k in range(1, MP):
            arrive(r.rp.at[k], r.m_hz, (k,))
            total = total + r.rp[k].astype(F32)
        r.proj_grad[...] = total.T
        dp_wait(r.sd, r.m_s3)
        for i in range(E // KE):
            r.phi_grad[i * KE : (i + 1) * KE, :] = r.sd[i]
        total = units[0].total()
        for k in range(1, MP):
            arrive(r.rq.at[k], r.m_gz, (k,))
            total = total + r.rq[k].astype(F32)
        for c in range(3):
            r.qkv_grad[c] = total[:, c * CW : (c + 1) * CW]
        for k in range(1, MP):
            arrive(r.tc.at[mp_at(k)], r.m_t2, (k,))
        r.norm_grad[...] = jnp.concatenate([sum_of(r.tc, MP), r.sd[E // KE, 0:2, :]], axis=0)
    else:
        r.norm_grad[...] = jnp.concatenate([rows1, rows2], axis=0)
    swap_wait(r.iin, r.m_ings)

    for wait in sends:
        wait()


def from_images(source):
    images = [source[i, 0:SEQ, :].astype(F32) for i in range(source.shape[0])]
    return jnp.concatenate(images, axis=0).T


def finish_kernel(passed, slots, dpre, hidden, dresults, iin, *refs):
    sources, (in_grad, out_grad, input_grad), rest = refs[:passed], refs[passed : passed + 3], refs[passed + 3 :]
    targets, (grads_in, grads_out, grad_t, sem, tile_sem) = rest[:passed], rest[passed:]
    copies = [pltpu.make_async_copy(a, b, sem.at[i]) for i, (a, b) in enumerate(zip(sources, targets))]
    for copy in copies:
        copy.start()
    experts, _, width = slots.shape
    tile = 256 if width % 256 == 0 else width
    count = 0
    for e in range(experts):
        for left, right, held, target in ((slots, dpre, grads_in, in_grad), (hidden, dresults, grads_out, out_grad)):
            for t in range(width // tile):
                here = pl.ds(t * tile, tile)
                held[e, here, :] = tn(left[e, :, t * tile : (t + 1) * tile], right[e])
                copy = pltpu.make_async_copy(held.at[e, here], target.at[e, here], tile_sem.at[count])
                copy.start()
                copies.append(copy)
                count += 1
    grad_t[...] = from_images(iin)
    last = pltpu.make_async_copy(grad_t, input_grad, sem.at[passed])
    last.start()
    for copy in copies + [last]:
        copy.wait()


def per_device(mesh, tokens, norm_params, w_qkv, w_proj, phi, w_in, w_out, cotangent):
    z = Sizes(mesh, tokens, w_qkv, phi, w_in)
    vmem, anyspace = pl.BlockSpec(memory_space=pltpu.VMEM), pl.BlockSpec(memory_space=pl.ANY)
    inputs = dict(
        tokens=tokens.T, norm_params=norm_params, w_qkv=w_qkv, w_proj=w_proj, phi=phi.T, cotangent=cotangent.T
    )
    specs = [vmem] * len(inputs)
    inputs.update(w_in=w_in, w_out=w_out)
    specs += [anyspace] * 2
    images = z.MP * z.DP
    outs = dict(
        output=((z.CW, z.ROWS), F32), iin=((z.MP, z.SP, z.CW), BF),
        phi_grad=((z.E, z.D), F32), norm_grad=((4, z.D), F32),
        slots=((z.EPD, images, z.D), BF), dresults=((z.EPD, images, z.D), BF),
        hidden=((z.EPD, images, z.F), BF), dpre=((z.EPD, images, z.F), BF),
    )
    if z.own_weights:
        outs.update(qkv_grad=((3, z.RB, z.CW), F32), proj_grad=((z.CW, z.RB), F32))
    else:
        outs.update(gq=((z.MP, z.D, z.QW), BF), gp=((z.D, z.D), BF))
        wall = lax.all_gather(w_qkv.astype(BF), "dp", axis=1, tiled=True)
        wall = jnp.concatenate([wall[c] for c in range(3)], axis=1)
        wpall = lax.all_gather(w_proj.T.astype(BF), "dp", axis=0, tiled=True)
        inputs.update(wall=lax.all_gather(wall, "mp"), wpall=lax.all_gather(wpall, "mp"))
        specs += [vmem] * 2
    names, scratch = scratch_of(z)
    result = pl.pallas_call(
        functools.partial(block_kernel, z, list(inputs), list(outs), names),
        out_shape=[jax.ShapeDtypeStruct(*one) for one in outs.values()],
        in_specs=specs,
        out_specs=[vmem] * len(outs),
        scratch_shapes=scratch,
        compiler_params=pltpu.CompilerParams(
            collective_id=0, has_side_effects=True, vmem_limit_bytes=62 * 2**20
        ),
        name="block",
    )(*inputs.values())
    got = dict(zip(outs, result))

    passed = ["output", "norm_grad", "phi_grad"] + (["qkv_grad", "proj_grad"] if z.own_weights else [])
    tile = 256 if z.F % 256 == 0 and z.D == z.F else z.F
    tiles = 2 * z.EPD * (z.F // tile)
    results = pl.pallas_call(
        functools.partial(finish_kernel, len(passed)),
        in_specs=[vmem] * (5 + len(passed)),
        out_specs=[anyspace] * (3 + len(passed)),
        out_shape=[
            jax.ShapeDtypeStruct((z.EPD, z.D, z.F), F32),
            jax.ShapeDtypeStruct((z.EPD, z.F, z.D), F32),
            jax.ShapeDtypeStruct((z.CW, z.ROWS), F32),
        ]
        + [jax.ShapeDtypeStruct(*outs[name]) for name in passed],
        scratch_shapes=[
            pltpu.VMEM((z.EPD, z.D, z.F), F32),
            pltpu.VMEM((z.EPD, z.F, z.D), F32),
            pltpu.VMEM((z.CW, z.ROWS), F32),
            pltpu.SemaphoreType.DMA((len(passed) + 1,)),
            pltpu.SemaphoreType.DMA((tiles,)),
        ],
        compiler_params=pltpu.CompilerParams(vmem_limit_bytes=60 * 2**20),
        name="finish",
    )(got["slots"], got["dpre"], got["hidden"], got["dresults"], got["iin"], *(got[name] for name in passed))
    in_grad, out_grad, input_grad = results[:3]
    got.update(zip(passed, results[3:]))
    output, input_grad = got["output"].T, input_grad.T
    phi_grad, norm_grad = got["phi_grad"].T, got["norm_grad"]
    if z.own_weights:
        qkv_grad, proj_grad = got["qkv_grad"], got["proj_grad"]
    else:
        phi_grad, norm_grad = lax.psum((phi_grad, norm_grad), ("dp", "mp"))
        gq = lax.psum_scatter(got["gq"].astype(F32), "mp", scatter_dimension=0, tiled=False)
        gp = lax.psum_scatter(got["gp"].astype(F32), "mp", scatter_dimension=1, tiled=True)
        gq = jnp.stack([gq[:, c * z.CW : (c + 1) * z.CW] for c in range(3)])
        qkv_grad = lax.psum_scatter(gq, "dp", scatter_dimension=1, tiled=True)
        proj_grad = lax.psum_scatter(gp, "dp", scatter_dimension=0, tiled=True).T
    return (
        output, input_grad, qkv_grad, proj_grad, in_grad, out_grad, phi_grad, norm_grad
    )


def solution(mesh):
    return jax.shard_map(
        functools.partial(per_device, mesh),
        mesh=mesh,
        in_specs=(
            P("dp", "mp"), P(), P(None, "dp", "mp"), P("mp", "dp"), P(),
            P("dp", None, "mp"), P("dp", "mp", None), P("dp", "mp"),
        ),
        out_specs=(
            P("dp", "mp"), P("dp", "mp"), P(None, "dp", "mp"), P("mp", "dp"),
            P("dp", None, "mp"), P("dp", "mp", None), P(), P(),
        ),
        check_vma=False,
    )
```

time: 161 us -> 116 us (0.72)
  Pallas kernels: 144 us -> 115 us
  local copies, waits for them, and re-layouts: 16 us -> 0 us
    pallas_call x1, Pallas kernels: 138 us -> 109 us  [per_device(): pl.pallas_call(functools.partial(block_kernel, z, list(inputs), list(outs...]
    unnamed x9 -> x0, local copies, waits for them, and re-layouts: 16 us -> none
where the time goes in v2:
time: 116 us
  Pallas kernels  115 us (99%)
    pallas_call x1, Pallas kernels, per_device(): pl.pallas_call(functools.partial(block_kernel, z, list(inputs), list(outs...  109 us
    pallas_call x1, Pallas kernels, per_device(): pl.pallas_call(functools.partial(finish_kernel, len(passed)), in_specs=[v...  5.81 us

profile of v2, /device:TPU:0, one launch (start us, length us, event | category | flops | bytes accessed | tf_op | source)
XLA Modules:
  0.0 115.7 jit_solution(6155124808510693335)
XLA Ops:
  0.6 109.0 %block.1 = (f32[192,784]{1,0:T(8,128)}, bf16[4,208,192]{2,1,0:T(8,128)(2,1)}, f32[16,768]{1,0:T(8,128)}, f32[4,768]{1,0:T(4,128)}, bf16[2,32,768]{2,1,0:T(8,128)...) custom-call(bf16[192,784]{1,0:T(8,128)(2,1)} %bitcast.6, ...), custom_call_target="tpu_custom_call" | custom-call | tf_op jit(solution)/shard_map/block/pallas_call | solution.py:721
  109.7 5.8 %finish.1 = (f32[2,768,768]{2,1,0:T(8,128)}, f32[2,768,768]{2,1,0:T(8,128)}, f32[192,784]{1,0:T(8,128)}, f32[192,784]{1,0:T(8,128)}, f32[4,768]{1,0:T(4,128)}, /...) custom-call(bf16[2,32,768]{2,1,0:T(8,128)(2,1)} %get-tuple-element.26.slots, ...), custom_call_target="tpu_custom_call" | custom-call | tf_op jit(solution)/shard_map/finish/pallas_call | solution.py:737

commit v3 on v2

--- a/solution.py
+++ b/solution.py
@@ -78,7 +78,7 @@
         self.SP = (SEQ + 15) // 16 * 16
         self.ROWS = tokens.shape[0]
         self.KE = 2 * self.EPD
-        self.own_weights = self.NX == 4 and self.RB % 32 == 0 and self.E + 2 <= self.KE * self.DP
+        self.own_weights = self.MP == 4 and self.NX == 4 and self.RB % 32 == 0 and self.E + 2 <= self.KE * self.DP
 
 
 def scratch_of(z):
@@ -107,21 +107,20 @@
     )
     if z.own_weights:
         items.update(
-            wall=v((MP, NX, IN, RB, QW), BF), wpall=v((MP, NX, IN, RB, CW), BF),
+            wall=v((MP, NX, IN, RB, D), BF),
             gq=v((MP, NX, IN, RB, QW), BF), gp=v((NX, IN, RB, D), BF),
             cq=v((MP, NX, RB, QW), BF), cp=v((NX, RB, D), BF),
             xq=v((MP, NX, RB, QW), BF), xp=v((NX, RB, D), BF),
             aq=v((MP, 4, half, QW), BF), ap=v((4, half, D), BF),
             bq=v((MP, 2, half, QW), BF), bp=v((2, half, D), BF),
             dq=v((MP, 2, half, QW), BF), dp_=v((2, half, D), BF),
-            zq=v((MP, RB, QW), BF), rq=v((MP, RB, QW), BF),
-            fp=v((MP, RB, CW), F32), zp=v((MP, RB, CW), BF), rp=v((MP, RB, CW), BF),
+            zf=v((RB, D), F32), zs=v((MP, RB, D), BF), zr=v((5, RB, D), BF), fp=v((MP, RB, CW), F32),
             sa=v((DP, KE, D), F32), sb=v((DP, KE, D), F32), sc=v((MP, KE, D), F32), sd=v((DP, KE, D), F32),
             ta=v((2, D), F32), tb=v((DP, 2, D), F32), tc=v((MP, 2, D), F32),
         )
         sems.update(
-            wz=(2, MP), wx=(2, MP, 4), wc=(2, MP), vz=(2, MP), vx=(2, 4), vc=(2,),
-            gc=(2, MP), gx=(2, MP, 6), gz=(2, MP), hc=(2,), hx=(2, 6), hz=(2, MP),
+            wz=(2, 5), wx=(2, MP, 4), wc=(2, MP),
+            gc=(2, MP), gx=(2, MP, 6), gz=(2, 5), hc=(2,), hx=(2, 6),
             s1=(2, DP), s2=(2, MP), s3=(2, DP), t1=(2, DP), t2=(2, MP),
         )
     names, shapes = [], []
@@ -167,7 +166,12 @@
         remote(ref, ref, sem, at, at, to_mp(1)).wait_recv()
 
     def mp_at(k):
-        return lax.rem(mp + k, MP)
+        if MP != 4:
+            return lax.rem(mp + k, MP)
+        return 2 * lax.rem(mp // 2 + k // 2, 2) + lax.rem(mp + k, 2)
+
+    def mp_back(k):
+        return k if MP == 4 else MP - k
 
     def dp_at(k):
         return lax.rem(dp + k, DP)
@@ -189,8 +193,9 @@
     load_out.start()
 
     if z.own_weights:
-        r.wall[mp, xy, co] = jnp.concatenate([r.w_qkv[c].astype(BF) for c in range(3)], axis=1)
-        r.wpall[mp, xy, co] = r.w_proj[...].T.astype(BF)
+        r.wall[mp, xy, co] = jnp.concatenate(
+            [r.w_qkv[c].astype(BF) for c in range(3)] + [r.w_proj[...].T.astype(BF)], axis=1
+        )
     pl.semaphore_wait(barrier, MP - 1 + DP - 1)
 
     def to_images(source, target):
@@ -201,7 +206,7 @@
 
     def swap(src, dst, sem):
         for k in range(1, MP):
-            send(src.at[mp_at(k)], dst.at[mp], sem, (k,), (MP - k,), to_mp(k))
+            send(src.at[mp_at(k)], dst.at[mp], sem, (k,), (mp_back(k),), to_mp(k))
         dst[mp] = src[mp]
 
     def swap_wait(dst, sem):
@@ -210,7 +215,7 @@
 
     def to_column(block, sem):
         for k in range(1, MP):
-            send(block, block, sem, (k,), (MP - k,), to_mp(k))
+            send(block, block, sem, (k,), (mp_back(k),), to_mp(k))
 
     class Plane:
         def __init__(self, block, sem, at):
@@ -233,55 +238,60 @@
             arrive(self.block(dg, 0, half), self.sem, self.at + (2,))
             arrive(self.block(dg, half, half), self.sem, self.at + (3,))
 
-    def qkv_plane(j):
-        return Plane(lambda pos, low, rows: r.wall.at[mp_at(j), pos, co, pl.ds(low, rows)], r.m_wx, (j,))
-
-    def other_core(ref, core, sem, at):
-        send(ref(core), ref(core), sem, at, at, to_core)
-
-    def qkv_cores(j):
-        return lambda core: r.wall.at[mp_at(j), :, core]
+    middle = lax.rem((mp + 1) // 2, 2)
+    slots_at = [0, 1, 2 + middle, 3 - middle]
+
+    def column_copy(k, way, slot, target):
+        block = r.wall.at[mp_at(k), xy, co]
+        return remote(block, block, r.m_wz, (way,), (slot,), to_mp(target))
+
+    def column_send(*copy):
+        column_copy(*copy).start()
+        sends.append(lambda: column_copy(*copy).wait_send())
+
+    def column_pass(*copy):
+        pl.when(middle == 1)(lambda: column_copy(*copy).start())
+        sends.append(lambda: pl.when(middle == 1)(lambda: column_copy(*copy).wait_send()))
+
+    def weight_plane(s):
+        return Plane(lambda pos, low, rows: r.wall.at[mp_at(slots_at[s]), pos, co, pl.ds(low, rows)], r.m_wx, (s,))
 
     def load_expert(copy, wide, low):
         copy.wait()
         low[...] = wide[...].astype(BF)
 
     if z.own_weights:
-        planes = [qkv_plane(j) for j in range(MP)]
-        proj_plane = Plane(lambda pos, low, rows: r.wpall.at[:, pos, co, pl.ds(low, rows)], r.m_vx, ())
-
-        def column_arrived(j):
-            arrive(r.wall.at[mp_at(j), xy, co], r.m_wz, (j,))
-            planes[j].start()
-
-        def plane_arrived(j):
-            planes[j].wait()
-            other_core(qkv_cores(j), co, r.m_wc, (j,))
-
-        to_column(r.wall.at[mp, xy, co], r.m_wz)
+        planes = [weight_plane(s) for s in range(MP)]
+
+        def column_arrived(s, k, way, slot, target):
+            arrive(r.wall.at[mp_at(slots_at[s]), xy, co], r.m_wz, (slots_at[s],))
+            column_pass(k, way, slot, target)
+            planes[s].start()
+
+        def plane_arrived(s):
+            planes[s].wait()
+            block = r.wall.at[mp_at(slots_at[s]), :, co]
+            send(block, block, r.m_wc, (s,), (s,), to_core)
+
+        column_send(0, 0, 1, 1)
+        column_pass(0, 1, 3, 3)
         planes[0].start()
-        to_column(r.wpall.at[mp, xy, co], r.m_vz)
         to_images(r.tokens, r.tsend)
         load_expert(load_in, r.wf_in, r.wb_in)
-        column_arrived(1)
+        column_arrived(1, 1, 2, 2, 3)
         planes[0].forward()
-        column_arrived(2)
+        to_images(r.cotangent, r.csend)
+        column_arrived(2, 3, 3, 2, 1)
         planes[1].forward()
         plane_arrived(0)
-        column_arrived(3)
+        load_expert(load_out, r.wf_out, r.wb_out)
+        column_arrived(3, 2, 4, 3, 1)
         swap(r.tsend, r.tin, r.m_tok)
         planes[2].forward()
         plane_arrived(1)
-        for k in range(1, MP):
-            arrive(r.wpall.at[mp_at(k), xy, co], r.m_vz, (k,))
-        proj_plane.start()
-        to_images(r.cotangent, r.csend)
         planes[3].forward()
+        swap(r.csend, r.cin, r.m_cot)
         plane_arrived(2)
-        load_expert(load_out, r.wf_out, r.wb_out)
-        swap(r.csend, r.cin, r.m_cot)
-        proj_plane.forward()
-        plane_arrived(3)
     else:
         to_images(r.tokens, r.tsend)
         swap(r.tsend, r.tin, r.m_tok)
@@ -304,26 +314,22 @@
     key_ok = lax.broadcasted_iota(jnp.int32, (1, SP), 1) < SEQ
 
     def weight(m):
-        return r.wall[m].reshape(D, QW) if z.own_weights else r.wall[m]
+        return r.wall[m].reshape(D, D)[:, :QW] if z.own_weights else r.wall[m]
 
     def proj_weight(m):
-        return r.wpall[m].reshape(D, CW) if z.own_weights else r.wpall[m]
+        return r.wall[m].reshape(D, D)[:, QW:] if z.own_weights else r.wpall[m]
 
     def head_cols(qkv, h):
         return (qkv[:, c * CW + h * HEAD_DIM : c * CW + (h + 1) * HEAD_DIM] for c in range(3))
 
-    def heads_forward(j, carry):
-        m = mp_at(j)
+    def heads_forward(s):
+        m = mp_at(slots_at[s])
         if z.own_weights:
-            arrive(r.wall.at[m, :, 1 - co], r.m_wc, (j,))
-
-            @pl.when(j == MP - 1)
-            def _():
-                proj_plane.wait()
-                remote(r.wpall.at[:, :, co], r.wpall.at[:, :, co], r.m_vc, (), (), to_core).start()
-
+            arrive(r.wall.at[m, :, 1 - co], r.m_wc, (s,))
         qkv = nn(r.h1[...], weight(m)).astype(BF)
         r.qkv[m] = qkv
+        if z.own_weights and s == MP - 2:
+            plane_arrived(s + 1)
         attended = []
         for h in range(z.HL):
             query, key, value = head_cols(qkv, h)
@@ -334,12 +340,9 @@
             r.probs[m, h] = probs
             attended.append(nn(probs.astype(BF), value))
         r.att[m] = jnp.concatenate(attended, axis=1).astype(BF)
-        return carry
-
-    lax.fori_loop(0, MP, heads_forward, 0)
-    if z.own_weights:
-        sends.append(lambda: remote(r.wpall.at[:, :, co], r.wpall.at[:, :, co], r.m_vc, (), (), to_core).wait_send())
-        arrive(r.wpall.at[:, :, 1 - co], r.m_vc, ())
+
+    for s in range(MP):
+        heads_forward(s)
 
     resid = own_image(r.tin).astype(F32)
     for m in range(MP):
@@ -396,7 +399,7 @@
     for kind in range(2):
         for k in range(1, MP):
             block = kind_rows(r.slot_all.at[mp], kind)
-            send(block, block, r.m_mp1, (kind, k), (kind, MP - k), to_mp(k))
+            send(block, block, r.m_mp1, (kind, k), (kind, mp_back(k)), to_mp(k))
 
     def expert_rows(kind):
         for k in range(1, MP):
@@ -415,8 +418,8 @@
         r.psend[:, here, :] = r.part[:, here, :].astype(BF)
         for k in range(1, MP):
             send(
-                kind_rows(r.psend.at[mp_at(k)], kind), kind_rows(r.pin.at[MP - k], kind),
-                r.m_mp2, (kind, k), (kind, MP - k), to_mp(k),
+                kind_rows(r.psend.at[mp_at(k)], kind), kind_rows(r.pin.at[mp_back(k)], kind),
+                r.m_mp2, (kind, k), (kind, mp_back(k)), to_mp(k),
             )
 
     slopes, results_part = [], []
@@ -504,23 +507,57 @@
                 pieces.append(piece + self.second[i].astype(F32))
             return jnp.concatenate(pieces, axis=0)
 
-    def qkv_unit(j):
-        return Unit(
-            r.gq.at[mp_at(j)], r.cq.at[j], r.xq.at[j], r.aq.at[j], r.bq.at[j], r.dq.at[j], r.m_gc, r.m_gx, (j,)
-        )
-
-    def qkv_column(j):
-        r.zq[j] = units[j].total().astype(BF)
-        send(r.zq.at[j], r.rq.at[MP - j], r.m_gz, (j,), (MP - j,), to_mp(j))
-
-    def proj_column():
+    orders = [2 + middle, 3 - middle, 1, 0]
+
+    def qkv_unit(i):
+        m = mp_at(orders[i])
+        return Unit(r.gq.at[m], r.cq.at[i], r.xq.at[i], r.aq.at[i], r.bq.at[i], r.dq.at[i], r.m_gc, r.m_gx, (i,))
+
+    def column_slot(i):
+        return (i + 3 * middle,) if i < 2 else (2,)
+
+    def from_line(index):
+        arrive(r.zr.at[index], r.m_gz, (index,))
+        return r.zr[index].astype(F32)
+
+    def unit_total(i):
+        return jnp.concatenate([units[i].total(), r.fp[mp_at(orders[i])]], axis=1)
+
+    def column(i):
+        r.zf[...] = unit_total(i)
+
+        @pl.when(middle == 1)
+        def _():
+            r.zf[...] += from_line([0, 1, 4][i])
+
+        r.zs[i] = r.zf[...].astype(BF)
+        target = 1 if i == 2 else 1 + 2 * middle
+        at = column_slot(i)
+
+        def copy():
+            return pltpu.make_async_remote_copy(
+                src_ref=r.zs.at[i], dst_ref=r.zr.at[at[0]], send_sem=r.m_gz.at[0, i], recv_sem=r.m_gz.at[1, at[0]],
+                device_id=to_mp(target), device_id_type=MESH,
+            )
+
+        copy().start()
+        sends.append(lambda: copy().wait_send())
+
+    def column_own():
+        r.zf[...] = unit_total(MP - 1) + from_line(2)
+
+        @pl.when(middle == 1)
+        def _():
+            r.zf[...] += from_line(3)
+
+        for c in range(3):
+            r.qkv_grad[c] = r.zf[:, c * CW : (c + 1) * CW]
+        r.proj_grad[...] = r.zf[:, QW:].T
+
+    def proj_total():
         total = proj_unit.total()
         for m in range(MP):
-            piece = total[:, m * CW : (m + 1) * CW]
-            r.fp[m] = piece
-            r.zp[m] = piece.astype(BF)
-        for k in range(1, MP):
-            send(r.zp.at[mp_at(k)], r.rp.at[MP - k], r.m_hz, (k,), (MP - k,), to_mp(k))
+            r.fp[m] = total[:, m * CW : (m + 1) * CW]
 
     def sum_of(ref, count):
         total = ref[0]
@@ -546,7 +583,7 @@
         )
 
     if z.own_weights:
-        units = [qkv_unit(j) for j in range(MP)]
+        units = [qkv_unit(i) for i in range(MP)]
         proj_unit = Unit(r.gp, r.cp, r.xp, r.ap, r.bp, r.dp_, r.m_hc, r.m_hx, ())
         r.gp[...] = proj_part.reshape(NX, IN, RB, D)
         proj_unit.start()
@@ -565,8 +602,7 @@
     else:
         r.phi_grad[...] = tn(dlogits, h2)
 
-    def heads_backward(j):
-        m = mp_at(j)
+    def heads_backward(m):
         qkv, datt = r.qkv[m], r.datt[m]
         pieces = [[], [], []]
         for h in range(z.HL):
@@ -587,21 +623,16 @@
             r.gq[m] = piece
         return dqkv
 
-    order = list(range(1, MP)) + [0]
-    between = {0: [], 1: [], 2: [], 3: []}
-    if z.own_weights:
-        between = {
-            0: [proj_unit.plane],
-            1: [units[1].plane, proj_unit.forward],
-            2: [units[2].plane, units[1].forward, small_column],
-            3: [units[3].plane, units[2].forward, proj_column],
-        }
-    dh1 = None
-    for i, j in enumerate(order):
-        dqkv = heads_backward(j)
+    between = {}
+    if z.own_weights:
+        first, second, third, last = units
+        between = {0: [proj_unit.plane], 1: [first.plane], 2: [second.plane, proj_unit.forward], 3: [third.plane]}
+    for i in range(MP):
+        m = mp_at(orders[i] if MP == 4 else i)
+        dqkv = heads_backward(m)
         if z.own_weights:
-            units[j].start()
-        part = nt(dqkv, weight(mp_at(j)))
+            units[i].start()
+        part = nt(dqkv, weight(m))
         if i == 0:
             r.dh1[...] = part
         else:
@@ -609,48 +640,41 @@
         for step in between.get(i, []):
             step()
 
-    if z.own_weights:
-        units[0].plane()
     normed1, inv1 = normalize(own_image(r.tin).astype(F32))
     dh1 = r.dh1[...]
+    input_grad = r.dresid[...] + norm_backward(dh1, gain1, normed1, inv1)
+    for m in range(MP):
+        r.isend[m] = input_grad[:, m * CW : (m + 1) * CW].astype(BF)
+    swap(r.isend, r.iin, r.m_ings)
     rows1 = gains(dh1, normed1)
     if z.own_weights:
         r.ta[...] = rows1
         for k in range(1, DP):
             send(r.ta, r.tb.at[dp], r.m_t1, (k,), (DP - k,), to_dp(k))
         r.tb[dp] = rows1
-    input_grad = r.dresid[...] + norm_backward(dh1, gain1, normed1, inv1)
-    for m in range(MP):
-        r.isend[m] = input_grad[:, m * CW : (m + 1) * CW].astype(BF)
-    swap(r.isend, r.iin, r.m_ings)
-
-    if z.own_weights:
-        qkv_column(1)
-        units[3].forward()
+
+    if z.own_weights:
+        first.forward()
+        last.plane()
+        second.forward()
+        third.forward()
+        proj_total()
+        column(0)
+        last.forward()
+        small_column()
+        column(1)
         small_back()
-        qkv_column(2)
-        units[0].forward()
         dp_wait(r.tb, r.m_t1)
         r.tc[mp] = sum_of(r.tb, DP)
         to_column(r.tc.at[mp], r.m_t2)
     swap_wait(r.oin, r.m_outs)
     r.output[...] = from_images(r.oin)
     if z.own_weights:
-        qkv_column(3)
-        total = r.fp[mp]
-        for k in range(1, MP):
-            arrive(r.rp.at[k], r.m_hz, (k,))
-            total = total + r.rp[k].astype(F32)
-        r.proj_grad[...] = total.T
+        column(2)
         dp_wait(r.sd, r.m_s3)
         for i in range(E // KE):
             r.phi_grad[i * KE : (i + 1) * KE, :] = r.sd[i]
-        total = units[0].total()
-        for k in range(1, MP):
-            arrive(r.rq.at[k], r.m_gz, (k,))
-            total = total + r.rq[k].astype(F32)
-        for c in range(3):
-            r.qkv_grad[c] = total[:, c * CW : (c + 1) * CW]
+        column_own()
         for k in range(1, MP):
             arrive(r.tc.at[mp_at(k)], r.m_t2, (k,))
         r.norm_grad[...] = jnp.concatenate([sum_of(r.tc, MP), r.sd[E // KE, 0:2, :]], axis=0)

time: 116 us -> 109 us (0.940)
  Pallas kernels: 115 us -> 108 us
    pallas_call x1, Pallas kernels: 109 us -> 102 us  [per_device(): pl.pallas_call(functools.partial(block_kernel, z, list(inputs), list(outs...]
where the time goes in v3:
time: 109 us; the launch traced here: 108 us
  Pallas kernels  108 us (99%)
    pallas_call x1, Pallas kernels, per_device(): pl.pallas_call(functools.partial(block_kernel, z, list(inputs), list(outs...  102 us
    pallas_call x1, Pallas kernels, per_device(): pl.pallas_call(functools.partial(finish_kernel, len(passed)), in_specs=[v...  5.81 us

profile of v3, /device:TPU:0, one launch (start us, length us, event | category | flops | bytes accessed | tf_op | source)
XLA Modules:
  0.0 108.4 jit_solution(1441531870674810227)
XLA Ops:
  0.6 101.8 %block.1 = (f32[192,784]{1,0:T(8,128)}, bf16[4,208,192]{2,1,0:T(8,128)(2,1)}, f32[16,768]{1,0:T(8,128)}, f32[4,768]{1,0:T(4,128)}, bf16[2,32,768]{2,1,0:T(8,128)...) custom-call(bf16[192,784]{1,0:T(8,128)(2,1)} %bitcast.6, ...), custom_call_target="tpu_custom_call" | custom-call | tf_op jit(solution)/shard_map/block/pallas_call | solution.py:745
  102.4 5.8 %finish.1 = (f32[2,768,768]{2,1,0:T(8,128)}, f32[2,768,768]{2,1,0:T(8,128)}, f32[192,784]{1,0:T(8,128)}, f32[192,784]{1,0:T(8,128)}, f32[4,768]{1,0:T(4,128)}, /...) custom-call(bf16[2,32,768]{2,1,0:T(8,128)(2,1)} %get-tuple-element.26.slots, ...), custom_call_target="tpu_custom_call" | custom-call | tf_op jit(solution)/shard_map/finish/pallas_call | solution.py:761

commit v4 on v3

--- a/solution.py
+++ b/solution.py
@@ -30,7 +30,7 @@
 
 
 def each(low, high, body):
-    if high - low <= 8:
+    if high - low <= 32:
         for i in range(low, high):
             body(i)
     else:
@@ -78,6 +78,12 @@
         self.SP = (SEQ + 15) // 16 * 16
         self.ROWS = tokens.shape[0]
         self.KE = 2 * self.EPD
+        self.NS = self.DP * self.MP
+        self.LC = self.D // 128
+        self.Q = self.EPD * self.LC
+        self.QP = (self.Q + 15) // 16 * 16
+        self.GD = 8 if self.DP % 8 == 0 else self.DP
+        self.GS = self.GD * self.MP
         self.own_weights = self.MP == 4 and self.NX == 4 and self.RB % 32 == 0 and self.E + 2 <= self.KE * self.DP
 
 
@@ -96,14 +102,14 @@
         h1=v((SP, D), BF), qkv=v((MP, SP, QW), BF), probs=v((MP, z.HL, SP, SP), F32),
         att=v((MP, SP, CW), BF), datt=v((MP, SP, CW), BF),
         resid=v((SP, D), F32), dresid=v((SP, D), F32), dh1=v((SP, D), F32),
-        slot_out=v((DP, KE, D), F32), slot_in=v((DP, KE, D), F32),
-        slot_all=v((MP, KE * DP, D), BF),
-        part=v((MP, KE * DP, D), F32), psend=v((MP, KE * DP, D), BF), pin=v((MP, KE * DP, D), BF),
-        back_out=v((DP, KE, D), F32), back_in=v((DP, KE, D), F32),
+        slot_out=v((2, DP, z.QP, 128), BF), slot_in=v((2, z.NS, z.QP, 128), BF),
+        back_out=v((2, z.NS, z.QP, 128), BF), back_in=v((2, z.NS, z.QP, 128), BF),
+        pick_in=v((z.Q * z.GS, z.GS * z.QP), BF), pick_back=v((z.GS * z.QP, z.Q * z.GS), BF),
+        pick_sum=v((z.LC * z.GD * z.EPD, z.GS * z.QP), BF),
     )
     sems = dict(
         tok=(2, MP), cot=(2, MP), outs=(2, MP), ings=(2, MP), hbm=(2,),
-        dp1=(2, DP), mp1=(2, 2, MP), mp2=(2, 2, MP), dp2=(2, DP),
+        slot=(2, 2), back=(2, 2),
     )
     if z.own_weights:
         items.update(
@@ -130,6 +136,8 @@
     for name, shape in sems.items():
         names.append("m_" + name)
         shapes.append(dma(shape))
+    names.append("entered")
+    shapes.append(pltpu.SemaphoreType.REGULAR)
     return names, shapes
 
 
@@ -182,10 +190,18 @@
     def to_dp(k):
         return (dp_at(k), mp)
 
+    def to_any(k):
+        if isinstance(k, int):
+            return (dp_at(k // MP), lax.rem(mp + k % MP, MP))
+        return (dp_at(k // MP), lax.rem(mp + lax.rem(k, MP), MP))
+
     barrier = pltpu.get_barrier_semaphore()
-    for k in range(1, MP):
-        pl.semaphore_signal(barrier, inc=1, device_id=to_mp(k), device_id_type=MESH)
-    each(1, DP, lambda k: pl.semaphore_signal(barrier, inc=1, device_id=to_dp(k), device_id_type=MESH))
+    if z.own_weights:
+        for k in range(1, MP):
+            pl.semaphore_signal(barrier, inc=1, device_id=to_mp(k), device_id_type=MESH)
+        each(1, DP, lambda k: pl.semaphore_signal(barrier, inc=1, device_id=to_dp(k), device_id_type=MESH))
+    else:
+        each(1, z.NS, lambda k: pl.semaphore_signal(barrier, inc=1, device_id=to_any(k), device_id_type=MESH))
 
     load_in = pltpu.make_async_copy(r.w_in, r.wf_in, r.m_hbm.at[0])
     load_out = pltpu.make_async_copy(r.w_out, r.wf_out, r.m_hbm.at[1])
@@ -196,7 +212,10 @@
         r.wall[mp, xy, co] = jnp.concatenate(
             [r.w_qkv[c].astype(BF) for c in range(3)] + [r.w_proj[...].T.astype(BF)], axis=1
         )
-    pl.semaphore_wait(barrier, MP - 1 + DP - 1)
+    pl.semaphore_wait(barrier, MP - 1 + DP - 1 if z.own_weights else z.NS - 1)
+    if z.own_weights:
+        for k in range(1, MP):
+            pl.semaphore_signal(r.entered, inc=1, device_id=to_mp(k), device_id_type=MESH)
 
     def to_images(source, target):
         target[...] = jnp.zeros((MP, SP, CW), BF)
@@ -259,6 +278,19 @@
     def load_expert(copy, wide, low):
         copy.wait()
         low[...] = wide[...].astype(BF)
+
+
+    def make_picks():
+        GS, Q, QP, LC = z.GS, z.Q, z.QP, z.LC
+        r.pick_in[...] = select_rows(Q * GS, GS * QP, lambda row: (row % GS) * QP + row // GS)
+        r.pick_back[...] = select_rows(
+            GS * QP, Q * GS, lambda row: jnp.where(row % QP < Q, (row % QP) * GS + row // QP, -1)
+        )
+        shape = (LC * z.GD * EPD, GS * QP)
+        row, col = (lax.broadcasted_iota(jnp.int32, shape, i) for i in range(2))
+        expert, chunk = row % (z.GD * EPD), row // (z.GD * EPD)
+        wanted = (col // (QP * MP) == expert // EPD) & (col % QP == (expert % EPD) * LC + chunk)
+        r.pick_sum[...] = jnp.where(wanted, 1.0, 0.0).astype(BF)
 
     if z.own_weights:
         planes = [weight_plane(s) for s in range(MP)]
@@ -285,6 +317,7 @@
         planes[1].forward()
         plane_arrived(0)
         load_expert(load_out, r.wf_out, r.wb_out)
+        make_picks()
         column_arrived(3, 2, 4, 3, 1)
         swap(r.tsend, r.tin, r.m_tok)
         planes[2].forward()
@@ -299,6 +332,7 @@
         swap(r.csend, r.cin, r.m_cot)
         load_expert(load_in, r.wf_in, r.wb_in)
         load_expert(load_out, r.wf_out, r.wb_out)
+        make_picks()
 
     swap_wait(r.tin, r.m_tok)
     gain1, shift1 = r.norm_params[0:1, :], r.norm_params[1:2, :]
@@ -359,68 +393,88 @@
     grown = jnp.exp(logits - jnp.max(logits, axis=1, keepdims=True))
     combine = grown / jnp.sum(grown, axis=1, keepdims=True)
     dispatch_low, combine_low = dispatch.astype(BF), combine.astype(BF)
+    slots = tn(dispatch_low, h2).astype(BF)
+
+    GD, GS, Q, QP, LC = z.GD, z.GS, z.Q, z.QP, z.LC
+    groups = DP // GD
+    here = dp * MP + mp
+
+    def stack(rows):
+        return jnp.concatenate([rows[:, c * 128 : (c + 1) * 128] for c in range(LC)], axis=0)
+
+    def unstack(chunks):
+        count = chunks.shape[0] // LC
+        return jnp.concatenate([chunks[c * count : (c + 1) * count] for c in range(LC)], axis=1)
+
+    def exchange(source, dst, kind, sem):
+        def copy(k):
+            device = to_any(k)
+            return pltpu.make_async_remote_copy(
+                src_ref=source(*device), dst_ref=dst.at[kind, here], send_sem=sem.at[0, kind],
+                recv_sem=sem.at[1, kind], device_id=device, device_id_type=MESH,
+            )
+
+        each(1, z.NS, lambda k: copy(k).start())
+        all_of_them = dst.at[kind, pl.ds(0, z.NS - 1)]
+        sends.append(
+            lambda: pltpu.make_async_remote_copy(
+                src_ref=all_of_them, dst_ref=all_of_them, send_sem=sem.at[0, kind], recv_sem=sem.at[1, kind],
+                device_id=to_mp(1), device_id_type=MESH,
+            ).wait_send()
+        )
+
+    def exchange_wait(dst, kind, sem):
+        all_of_them = dst.at[kind, pl.ds(0, z.NS - 1)]
+        pltpu.make_async_remote_copy(
+            src_ref=all_of_them, dst_ref=all_of_them, send_sem=sem.at[0, kind], recv_sem=sem.at[1, kind],
+            device_id=to_mp(1), device_id_type=MESH,
+        ).wait_recv()
+
+    def out_row(row):
+        d, q = row // QP, row % QP
+        return jnp.where(q < Q, (q % LC) * (GD * EPD) + d * EPD + q // LC, -1)
+
+    pick_out = select_rows(GD * QP, LC * GD * EPD, out_row)
+
+    def send_slots(kind, rows):
+        for g in range(groups):
+            part = nn(pick_out, stack(rows[g * GD * EPD : (g + 1) * GD * EPD]))
+            r.slot_out[kind, g * GD : (g + 1) * GD] = part.astype(BF).reshape(GD, QP, 128)
+        exchange(lambda d, m: r.slot_out.at[kind, d], r.slot_in, kind, r.m_slot)
+        r.slot_in[kind, here] = r.slot_out[kind, dp]
+
+    if z.own_weights:
+        pl.semaphore_wait(r.entered, MP - 1)
+    send_slots(0, slots)
     swap_wait(r.cin, r.m_cot)
     grad = own_image(r.cin)
-    slots = tn(dispatch_low, h2).astype(BF)
-    dresults = tn(combine_low, grad).astype(BF)
-
-    def spread(target, rows):
-        for d in range(DP):
-            target[d] = rows[d * KE : (d + 1) * KE]
-
-    def collect(source):
-        return jnp.concatenate([source[d] for d in range(DP)], axis=0)
-
-    def dp_swap(src, dst, sem):
-        def copy(k):
-            return remote(src.at[dp_at(k)], dst.at[dp], sem, (k,), (DP - k,), to_dp(k))
-
-        each(1, DP, lambda k: copy(k).start())
-        sends.append(lambda: each(1, DP, lambda k: copy(k).wait_send()))
-        dst[dp] = src[dp]
-
-    def dp_wait(dst, sem):
-        each(1, DP, lambda k: arrive(dst.at[dp_at(k)], sem, (k,)))
-
-    def out_row(row):
-        d, q = row // KE, row % KE
-        return (q // EPD) * E + d * EPD + q % EPD
-
-    spread(r.slot_out, nn(select_rows(DP * KE, 2 * E, out_row), jnp.concatenate([slots, dresults], axis=0)))
-    dp_swap(r.slot_out, r.slot_in, r.m_dp1)
-    dp_wait(r.slot_in, r.m_dp1)
-    gather_rows = select_rows(KE * DP, DP * KE, lambda row: (row % DP) * KE + row // DP)
-    r.slot_all[mp] = nn(gather_rows, collect(r.slot_in).astype(BF)).astype(BF)
-    rows = EPD * DP
-
-    def kind_rows(ref, kind):
-        return ref.at[pl.ds(kind * rows, rows)]
-
-    for kind in range(2):
-        for k in range(1, MP):
-            block = kind_rows(r.slot_all.at[mp], kind)
-            send(block, block, r.m_mp1, (kind, k), (kind, mp_back(k)), to_mp(k))
+    send_slots(1, tn(combine_low, grad).astype(BF))
 
     def expert_rows(kind):
-        for k in range(1, MP):
-            arrive(kind_rows(r.slot_all.at[mp_at(k)], kind), r.m_mp1, (kind, k))
-        parts = [r.slot_all[m, kind * rows : (kind + 1) * rows, :].astype(F32) for m in range(MP)]
-        return [
-            jnp.concatenate([one[e * DP : (e + 1) * DP] for one in parts], axis=0).astype(BF) for e in range(EPD)
-        ]
+        exchange_wait(r.slot_in, kind, r.m_slot)
+        found = [[] for _ in range(EPD)]
+        for g in range(groups):
+            got = r.slot_in[kind, g * GS : (g + 1) * GS].reshape(GS * QP, 128)
+            chunks = nn(r.pick_in[...], got)
+            for e in range(EPD):
+                found[e].append(unstack(chunks[e * LC * GS : (e + 1) * LC * GS]).astype(BF))
+        return [jnp.concatenate(one, axis=0) for one in found]
 
     def send_parts(kind, per_expert):
-        for e in range(EPD):
-            at = kind * rows + e * DP
-            for m in range(MP):
-                r.part[m, at : at + DP, :] = per_expert[e][m * DP : (m + 1) * DP]
-        here = slice(kind * rows, (kind + 1) * rows)
-        r.psend[:, here, :] = r.part[:, here, :].astype(BF)
-        for k in range(1, MP):
-            send(
-                kind_rows(r.psend.at[mp_at(k)], kind), kind_rows(r.pin.at[mp_back(k)], kind),
-                r.m_mp2, (kind, k), (kind, mp_back(k)), to_mp(k),
-            )
+        for g in range(groups):
+            rows = [stack(one[g * GS : (g + 1) * GS]).astype(BF) for one in per_expert]
+            part = nn(r.pick_back[...], jnp.concatenate(rows, axis=0))
+            r.back_out[kind, g * GS : (g + 1) * GS] = part.astype(BF).reshape(GS, QP, 128)
+        exchange(lambda d, m: r.back_out.at[kind, d * MP + m], r.back_in, kind, r.m_back)
+        r.back_in[kind, here] = r.back_out[kind, here]
+
+    def back_rows(kind):
+        exchange_wait(r.back_in, kind, r.m_back)
+        found = []
+        for g in range(groups):
+            got = r.back_in[kind, g * GS : (g + 1) * GS].reshape(GS * QP, 128)
+            found.append(unstack(nn(r.pick_sum[...], got)).astype(BF))
+        return jnp.concatenate(found, axis=0)
 
     slopes, results_part = [], []
     for e, slots_e in enumerate(expert_rows(0)):
@@ -437,27 +491,13 @@
         dslots_part.append(nt(dpre, r.wb_in[e]))
         r.dresults[e], r.dpre[e] = dresults_e, dpre
     send_parts(1, dslots_part)
-    total = r.part[mp]
-    for k in range(1, MP):
-        for kind in range(2):
-            arrive(kind_rows(r.pin.at[k], kind), r.m_mp2, (kind, k))
-        total = total + r.pin[k].astype(F32)
-    back_rows = select_rows(DP * KE, KE * DP, lambda row: (row % KE) * DP + row // KE)
-    spread(r.back_out, nn(back_rows, total.astype(BF)))
-    dp_swap(r.back_out, r.back_in, r.m_dp2)
-    dp_wait(r.back_in, r.m_dp2)
-
-    def result_row(row):
-        kind, e = row // E, row % E
-        return (e // EPD) * KE + kind * EPD + e % EPD
-
-    both = nn(select_rows(2 * E, DP * KE, result_row), collect(r.back_in).astype(BF)).astype(BF)
-    results, dslots = both[:E], both[E:]
+    results = back_rows(0)
 
     output = r.resid[...] + nn(combine_low, results)
     for m in range(MP):
         r.osend[m] = output[:, m * CW : (m + 1) * CW].astype(BF)
     swap(r.osend, r.oin, r.m_outs)
+    dslots = back_rows(1)
     dcombine, ddispatch = nt(grad, results), nt(h2, dslots)
     dlogits = dispatch * (ddispatch - jnp.sum(dispatch * ddispatch, axis=0, keepdims=True))
     dlogits = dlogits + combine * (dcombine - jnp.sum(combine * dcombine, axis=1, keepdims=True))
@@ -558,6 +598,17 @@
         total = proj_unit.total()
         for m in range(MP):
             r.fp[m] = total[:, m * CW : (m + 1) * CW]
+
+    def dp_swap(src, dst, sem):
+        def copy(k):
+            return remote(src.at[dp_at(k)], dst.at[dp], sem, (k,), (DP - k,), to_dp(k))
+
+        each(1, DP, lambda k: copy(k).start())
+        sends.append(lambda: each(1, DP, lambda k: copy(k).wait_send()))
+        dst[dp] = src[dp]
+
+    def dp_wait(dst, sem):
+        each(1, DP, lambda k: arrive(dst.at[dp_at(k)], sem, (k,)))
 
     def sum_of(ref, count):
         total = ref[0]

time: 109 us -> 106 us (0.972)
  Pallas kernels: 108 us -> 105 us
    pallas_call x1, Pallas kernels: 102 us -> 98.8 us  [per_device(): pl.pallas_call(functools.partial(block_kernel, z, list(inputs), list(outs...]
where the time goes in v4:
time: 106 us; the launch traced here: 105 us
  Pallas kernels  105 us (99%)
    pallas_call x1, Pallas kernels, per_device(): pl.pallas_call(functools.partial(block_kernel, z, list(inputs), list(outs...  98.8 us
    pallas_call x1, Pallas kernels, per_device(): pl.pallas_call(functools.partial(finish_kernel, len(passed)), in_specs=[v...  5.81 us

profile of v4, /device:TPU:0, one launch (start us, length us, event | category | flops | bytes accessed | tf_op | source)
XLA Modules:
  0.0 105.4 jit_solution(11012906505488946503)
XLA Ops:
  0.6 98.8 %block.1 = (f32[192,784]{1,0:T(8,128)}, bf16[4,208,192]{2,1,0:T(8,128)(2,1)}, f32[16,768]{1,0:T(8,128)}, f32[4,768]{1,0:T(4,128)}, bf16[2,32,768]{2,1,0:T(8,128)...) custom-call(bf16[192,784]{1,0:T(8,128)(2,1)} %bitcast.6, ...), custom_call_target="tpu_custom_call" | custom-call | tf_op jit(solution)/shard_map/block/pallas_call | solution.py:796
  99.4 5.8 %finish.1 = (f32[2,768,768]{2,1,0:T(8,128)}, f32[2,768,768]{2,1,0:T(8,128)}, f32[192,784]{1,0:T(8,128)}, f32[192,784]{1,0:T(8,128)}, f32[4,768]{1,0:T(4,128)}, /...) custom-call(bf16[2,32,768]{2,1,0:T(8,128)(2,1)} %get-tuple-element.26.slots, ...), custom_call_target="tpu_custom_call" | custom-call | tf_op jit(solution)/shard_map/finish/pallas_call | solution.py:812

commit v5 on v4

--- a/solution.py
+++ b/solution.py
@@ -297,7 +297,8 @@
 
         def column_arrived(s, k, way, slot, target):
             arrive(r.wall.at[mp_at(slots_at[s]), xy, co], r.m_wz, (slots_at[s],))
-            column_pass(k, way, slot, target)
+            if k:
+                column_pass(k, way, slot, target)
             planes[s].start()
 
         def plane_arrived(s):
@@ -306,7 +307,7 @@
             send(block, block, r.m_wc, (s,), (s,), to_core)
 
         column_send(0, 0, 1, 1)
-        column_pass(0, 1, 3, 3)
+        column_send(0, 1, 3, 3)
         planes[0].start()
         to_images(r.tokens, r.tsend)
         load_expert(load_in, r.wf_in, r.wb_in)
@@ -315,11 +316,11 @@
         to_images(r.cotangent, r.csend)
         column_arrived(2, 3, 3, 2, 1)
         planes[1].forward()
+        swap(r.tsend, r.tin, r.m_tok)
         plane_arrived(0)
         load_expert(load_out, r.wf_out, r.wb_out)
         make_picks()
-        column_arrived(3, 2, 4, 3, 1)
-        swap(r.tsend, r.tin, r.m_tok)
+        column_arrived(3, 0, 0, 0, 0)
         planes[2].forward()
         plane_arrived(1)
         planes[3].forward()

time: 106 us -> 103 us (0.972)
  Pallas kernels: 105 us -> 102 us
    pallas_call x1, Pallas kernels: 98.8 us -> 95.8 us  [per_device(): pl.pallas_call(functools.partial(block_kernel, z, list(inputs), list(outs...]
where the time goes in v5:
time: 103 us; the launch traced here: 102 us
  Pallas kernels  102 us (99%)
    pallas_call x1, Pallas kernels, per_device(): pl.pallas_call(functools.partial(block_kernel, z, list(inputs), list(outs...  95.8 us
    pallas_call x1, Pallas kernels, per_device(): pl.pallas_call(functools.partial(finish_kernel, len(passed)), in_specs=[v...  5.81 us

profile of v5, /device:TPU:0, one launch (start us, length us, event | category | flops | bytes accessed | tf_op | source)
XLA Modules:
  0.0 102.4 jit_solution(14711441051708636924)
XLA Ops:
  0.6 95.8 %block.1 = (f32[192,784]{1,0:T(8,128)}, bf16[4,208,192]{2,1,0:T(8,128)(2,1)}, f32[16,768]{1,0:T(8,128)}, f32[4,768]{1,0:T(4,128)}, bf16[2,32,768]{2,1,0:T(8,128)...) custom-call(bf16[192,784]{1,0:T(8,128)(2,1)} %bitcast.6, ...), custom_call_target="tpu_custom_call" | custom-call | tf_op jit(solution)/shard_map/block/pallas_call | solution.py:797
  96.4 5.8 %finish.1 = (f32[2,768,768]{2,1,0:T(8,128)}, f32[2,768,768]{2,1,0:T(8,128)}, f32[192,784]{1,0:T(8,128)}, f32[192,784]{1,0:T(8,128)}, f32[4,768]{1,0:T(4,128)}, /...) custom-call(bf16[2,32,768]{2,1,0:T(8,128)(2,1)} %get-tuple-element.26.slots, ...), custom_call_target="tpu_custom_call" | custom-call | tf_op jit(solution)/shard_map/finish/pallas_call | solution.py:813

commit v6 on v5

--- a/solution.py
+++ b/solution.py
@@ -107,12 +107,18 @@
         pick_in=v((z.Q * z.GS, z.GS * z.QP), BF), pick_back=v((z.GS * z.QP, z.Q * z.GS), BF),
         pick_sum=v((z.LC * z.GD * z.EPD, z.GS * z.QP), BF),
     )
+    items.update(
+        tokens=v((CW, z.ROWS), BF), cotangent=v((CW, z.ROWS), BF), norm_params=v((4, D), F32), phi=v((z.E, D), F32),
+        output=v((CW, z.ROWS), F32), slots=v((z.EPD, z.NS, D), BF), dresults=v((z.EPD, z.NS, D), BF),
+        hidden=v((z.EPD, z.NS, z.F), BF), dpre=v((z.EPD, z.NS, z.F), BF),
+    )
     sems = dict(
-        tok=(2, MP), cot=(2, MP), outs=(2, MP), ings=(2, MP), hbm=(2,),
+        load=(6,), store=(5,), tok=(2, MP), cot=(2, MP), outs=(2, MP), ings=(2, MP), hbm=(2,),
         slot=(2, 2), back=(2, 2),
     )
     if z.own_weights:
         items.update(
+            w_qkv=v((3, RB, CW), F32), w_proj=v((CW, RB), F32),
             wall=v((MP, NX, IN, RB, D), BF),
             gq=v((MP, NX, IN, RB, QW), BF), gp=v((NX, IN, RB, D), BF),
             cq=v((MP, NX, RB, QW), BF), cp=v((NX, RB, D), BF),
@@ -203,12 +209,25 @@
     else:
         each(1, z.NS, lambda k: pl.semaphore_signal(barrier, inc=1, device_id=to_any(k), device_id_type=MESH))
 
+    loads, stores = {}, []
+    needed = (["w_qkv", "w_proj"] if z.own_weights else []) + ["tokens", "cotangent", "norm_params", "phi"]
+    for i, name in enumerate(needed):
+        loads[name] = pltpu.make_async_copy(getattr(r, "hbm_" + name), getattr(r, name), r.m_load.at[i])
+        loads[name].start()
+
+    def store(name):
+        copy = pltpu.make_async_copy(getattr(r, name), getattr(r, "hbm_" + name), r.m_store.at[len(stores)])
+        copy.start()
+        stores.append(copy)
+
     load_in = pltpu.make_async_copy(r.w_in, r.wf_in, r.m_hbm.at[0])
     load_out = pltpu.make_async_copy(r.w_out, r.wf_out, r.m_hbm.at[1])
     load_in.start()
     load_out.start()
 
     if z.own_weights:
+        loads["w_qkv"].wait()
+        loads["w_proj"].wait()
         r.wall[mp, xy, co] = jnp.concatenate(
             [r.w_qkv[c].astype(BF) for c in range(3)] + [r.w_proj[...].T.astype(BF)], axis=1
         )
@@ -309,10 +328,12 @@
         column_send(0, 0, 1, 1)
         column_send(0, 1, 3, 3)
         planes[0].start()
+        loads["tokens"].wait()
         to_images(r.tokens, r.tsend)
         load_expert(load_in, r.wf_in, r.wb_in)
         column_arrived(1, 1, 2, 2, 3)
         planes[0].forward()
+        loads["cotangent"].wait()
         to_images(r.cotangent, r.csend)
         column_arrived(2, 3, 3, 2, 1)
         planes[1].forward()
@@ -327,8 +348,10 @@
         swap(r.csend, r.cin, r.m_cot)
         plane_arrived(2)
     else:
+        loads["tokens"].wait()
         to_images(r.tokens, r.tsend)
         swap(r.tsend, r.tin, r.m_tok)
+        loads["cotangent"].wait()
         to_images(r.cotangent, r.csend)
         swap(r.csend, r.cin, r.m_cot)
         load_expert(load_in, r.wf_in, r.wb_in)
@@ -336,6 +359,8 @@
         make_picks()
 
     swap_wait(r.tin, r.m_tok)
+    loads["norm_params"].wait()
+    loads["phi"].wait()
     gain1, shift1 = r.norm_params[0:1, :], r.norm_params[1:2, :]
     gain2, shift2 = r.norm_params[2:3, :], r.norm_params[3:4, :]
 
@@ -492,6 +517,8 @@
         dslots_part.append(nt(dpre, r.wb_in[e]))
         r.dresults[e], r.dpre[e] = dresults_e, dpre
     send_parts(1, dslots_part)
+    for name in ("slots", "hidden", "dresults", "dpre"):
+        store(name)
     results = back_rows(0)
 
     output = r.resid[...] + nn(combine_low, results)
@@ -716,13 +743,15 @@
         small_column()
         column(1)
         small_back()
+    if z.own_weights:
+        column(2)
         dp_wait(r.tb, r.m_t1)
         r.tc[mp] = sum_of(r.tb, DP)
         to_column(r.tc.at[mp], r.m_t2)
     swap_wait(r.oin, r.m_outs)
     r.output[...] = from_images(r.oin)
-    if z.own_weights:
-        column(2)
+    store("output")
+    if z.own_weights:
         dp_wait(r.sd, r.m_s3)
         for i in range(E // KE):
             r.phi_grad[i * KE : (i + 1) * KE, :] = r.sd[i]
@@ -736,6 +765,8 @@
 
     for wait in sends:
         wait()
+    for copy in stores:
+        copy.wait()
 
 
 def from_images(source):
@@ -774,15 +805,16 @@
     inputs = dict(
         tokens=tokens.T, norm_params=norm_params, w_qkv=w_qkv, w_proj=w_proj, phi=phi.T, cotangent=cotangent.T
     )
-    specs = [vmem] * len(inputs)
+    inputs = {"hbm_" + name: value for name, value in inputs.items()}
+    specs = [anyspace] * len(inputs)
     inputs.update(w_in=w_in, w_out=w_out)
     specs += [anyspace] * 2
     images = z.MP * z.DP
     outs = dict(
-        output=((z.CW, z.ROWS), F32), iin=((z.MP, z.SP, z.CW), BF),
+        hbm_output=((z.CW, z.ROWS), F32), iin=((z.MP, z.SP, z.CW), BF),
         phi_grad=((z.E, z.D), F32), norm_grad=((4, z.D), F32),
-        slots=((z.EPD, images, z.D), BF), dresults=((z.EPD, images, z.D), BF),
-        hidden=((z.EPD, images, z.F), BF), dpre=((z.EPD, images, z.F), BF),
+        hbm_slots=((z.EPD, images, z.D), BF), hbm_dresults=((z.EPD, images, z.D), BF),
+        hbm_hidden=((z.EPD, images, z.F), BF), hbm_dpre=((z.EPD, images, z.F), BF),
     )
     if z.own_weights:
         outs.update(qkv_grad=((3, z.RB, z.CW), F32), proj_grad=((z.CW, z.RB), F32))
@@ -798,13 +830,14 @@
         functools.partial(block_kernel, z, list(inputs), list(outs), names),
         out_shape=[jax.ShapeDtypeStruct(*one) for one in outs.values()],
         in_specs=specs,
-        out_specs=[vmem] * len(outs),
+        out_specs=[anyspace if name.startswith("hbm_") else vmem for name in outs],
         scratch_shapes=scratch,
         compiler_params=pltpu.CompilerParams(
             collective_id=0, has_side_effects=True, vmem_limit_bytes=62 * 2**20
         ),
         name="block",
     )(*inputs.values())
+    outs = {name.removeprefix("hbm_"): one for name, one in outs.items()}
     got = dict(zip(outs, result))
 
     passed = ["output", "norm_grad", "phi_grad"] + (["qkv_grad", "proj_grad"] if z.own_weights else [])

time: 103 us -> 102 us (level)
  no operation moved by 1% of the time
where the time goes in v6:
time: 102 us
  Pallas kernels  101 us (99%)
    pallas_call x1, Pallas kernels, per_device(): pl.pallas_call(functools.partial(block_kernel, z, list(inputs), list(outs...  95.2 us
    pallas_call x1, Pallas kernels, per_device(): pl.pallas_call(functools.partial(finish_kernel, len(passed)), in_specs=[v...  5.81 us

profile of v6, /device:TPU:0, one launch (start us, length us, event | category | flops | bytes accessed | tf_op | source)
XLA Modules:
  0.0 101.9 jit_solution(3956777808102312285)
XLA Ops:
  0.6 95.2 %block.1 = (f32[192,784]{1,0:T(8,128)}, bf16[4,208,192]{2,1,0:T(8,128)(2,1)}, f32[16,768]{1,0:T(8,128)}, f32[4,768]{1,0:T(4,128)}, bf16[2,32,768]{2,1,0:T(8,128)...) custom-call(bf16[192,784]{1,0:T(8,128)(2,1)} %bitcast.6, ...), custom_call_target="tpu_custom_call" | custom-call | tf_op jit(solution)/shard_map/block/pallas_call | solution.py:829
  95.9 5.8 %finish.1 = (f32[2,768,768]{2,1,0:T(8,128)}, f32[2,768,768]{2,1,0:T(8,128)}, f32[192,784]{1,0:T(8,128)}, f32[192,784]{1,0:T(8,128)}, f32[4,768]{1,0:T(4,128)}, /...) custom-call(bf16[2,32,768]{2,1,0:T(8,128)(2,1)} %get-tuple-element.26.slots, ...), custom_call_target="tpu_custom_call" | custom-call | tf_op jit(solution)/shard_map/finish/pallas_call | solution.py:846

commit v7 on v6

--- a/solution.py
+++ b/solution.py
@@ -388,8 +388,8 @@
             arrive(r.wall.at[m, :, 1 - co], r.m_wc, (s,))
         qkv = nn(r.h1[...], weight(m)).astype(BF)
         r.qkv[m] = qkv
-        if z.own_weights and s == MP - 2:
-            plane_arrived(s + 1)
+        if z.own_weights and s == MP - 3:
+            plane_arrived(MP - 1)
         attended = []
         for h in range(z.HL):
             query, key, value = head_cols(qkv, h)

time: 102 us -> 102 us (level)
  no operation moved by 1% of the time
where the time goes in v7:
time: 102 us; the launch traced here: 101 us
  Pallas kernels  101 us (99%)
    pallas_call x1, Pallas kernels, per_device(): pl.pallas_call(functools.partial(block_kernel, z, list(inputs), list(outs...  94.8 us
    pallas_call x1, Pallas kernels, per_device(): pl.pallas_call(functools.partial(finish_kernel, len(passed)), in_specs=[v...  5.81 us

profile of v7, /device:TPU:0, one launch (start us, length us, event | category | flops | bytes accessed | tf_op | source)
XLA Modules:
  0.0 101.4 jit_solution(12470098985796207879)
XLA Ops:
  0.6 94.8 %block.1 = (f32[192,784]{1,0:T(8,128)}, bf16[4,208,192]{2,1,0:T(8,128)(2,1)}, f32[16,768]{1,0:T(8,128)}, f32[4,768]{1,0:T(4,128)}, bf16[2,32,768]{2,1,0:T(8,128)...) custom-call(bf16[192,784]{1,0:T(8,128)(2,1)} %bitcast.6, ...), custom_call_target="tpu_custom_call" | custom-call | tf_op jit(solution)/shard_map/block/pallas_call | solution.py:829
  95.5 5.8 %finish.1 = (f32[2,768,768]{2,1,0:T(8,128)}, f32[2,768,768]{2,1,0:T(8,128)}, f32[192,784]{1,0:T(8,128)}, f32[192,784]{1,0:T(8,128)}, f32[4,768]{1,0:T(4,128)}, /...) custom-call(bf16[2,32,768]{2,1,0:T(8,128)(2,1)} %get-tuple-element.26.slots, ...), custom_call_target="tpu_custom_call" | custom-call | tf_op jit(solution)/shard_map/finish/pallas_call | solution.py:846
